TPU v7x, 256 devices: a whole 4x4x8 slice. The times are simulated.
256 devices in a mesh: band: 64 (over y, z, core), chan: 4 (over x).
Axes of the slice: x: 4, y: 4, z: 8, core: 2. Of those that a mesh axis runs over, the one named last changes fastest.
Arguments:
- grid_in: bfloat16 [474, 65536], P(None, 'band'), may hold values from -6 to 6
- w_grid: bfloat16 [474, 512], P(None, 'chan'), may hold values from -0.25 to 0.25
- mesh_in: bfloat16 [512, 32768], P('chan', 'band'), may hold values from -6 to 6
- g2m_attr: bfloat16 [4, 524288], P(None, 'band'), may hold values from -6 to 6
- g2m_send: int32 [320, 512], P('band'), may hold values from 0 to 1023
- g2m_src: int32 [524288], P('band'), may hold values from 0 to 2559, as said below
- g2m_dst: int32 [524288], P('band'), may hold values from -1 to 511, as said below
- w_gs: bfloat16 [512, 512], P(None, 'chan'), may hold values from -0.25 to 0.25
- w_gr: bfloat16 [512, 512], P(None, 'chan'), may hold values from -0.25 to 0.25
- w_ge: bfloat16 [4, 512], P(None, 'chan'), may hold values from -3 to 3
- w_nm: bfloat16 [512, 512], P('chan'), may hold values from -0.25 to 0.25
- w_na: bfloat16 [512, 512], P('chan'), may hold values from -0.09375 to 0.09375
- w_no: bfloat16 [512, 512], P('chan'), may hold values from -1.767767 to 1.767767
- gain_enc: float32 [512], P('chan'), may hold values from 0.1 to 1.9
- mesh_attr: bfloat16 [4, 262144], P(None, 'band'), may hold values from -6 to 6
- mesh_send: int32 [320, 256], P('band'), may hold values from 0 to 511
- mesh_src: int32 [262144], P('band'), may hold values from 0 to 1279, as said below
- mesh_dst: int32 [262144], P('band'), may hold values from 0 to 511, as said below
- w_ms: bfloat16 [512, 512], P(None, 'chan'), may hold values from -0.25 to 0.25
- w_mr: bfloat16 [512, 512], P(None, 'chan'), may hold values from -0.25 to 0.25
- w_me: bfloat16 [4, 512], P(None, 'chan'), may hold values from -3 to 3
- w_pm: bfloat16 [512, 512], P('chan'), may hold values from -0.25 to 0.25
- w_pa: bfloat16 [512, 512], P('chan'), may hold values from -0.125 to 0.125
- w_po: bfloat16 [512, 512], P('chan'), may hold values from -1.767767 to 1.767767
- gain_proc: float32 [512], P('chan'), may hold values from 0.1 to 1.9
- cotangent: bfloat16 [512, 32768], P('chan', 'band'), may hold values from -6 to 6
Outputs:
- mesh_out: bfloat16 [512, 32768], P('chan', 'band')
- mesh_grad: float32 [512, 32768], P('chan', 'band')
- w_grid_grad: float32 [474, 512], P(None, 'chan')
Inputs may be any that keep to these rules, and one draw needn't show every extreme that they name: `g2m_dst`: each device's 8192 slots hold its live edges first, sorted by receiver, then -1 in the rest; receivers 0 and 511 occur on every device; the first and last band devices are full, and every device has at least 819 live edges. `g2m_src`: column b names slot j = b // 512 of the device's table; live edges name only slots j whose source device d + 2 - j exists. `mesh_dst`: each device's 4096 edges are sorted by receiver; receivers 0 and 511 occur on every device. `mesh_src`: column b names slot j = b // 256; edges name only slots j whose source device d + 2 - j exists.
All inputs are finite; a program needn't handle non-finite values.
Results may differ from a plain program's by a relative error of at most 0.035.
Values may be sent and summed in bfloat16 or wider, within the bound.
A program may use at most 128 MiB of HBM per device.

v0:
```python
import jax
import jax.numpy as jnp
from jax import lax
from jax.sharding import PartitionSpec as P

eps = 1e-05


def from_behind(block, axis, distance):
    devices = range(lax.axis_size(axis))
    route = [(i - distance, i) for i in devices if i - distance in devices]
    return lax.ppermute(block, axis, route)


def silu_grad(values):
    sigmoid_v = jax.nn.sigmoid(values)
    return sigmoid_v * (1.0 + values * (1.0 - sigmoid_v))


def contract(weight, field_in):
    return lax.dot_general(
        weight, field_in, (((0,), (0,)), ((), ())), preferred_element_type=jnp.float32
    )


def expand(weight, grad_in):
    return jnp.dot(weight, grad_in, preferred_element_type=jnp.float32)


def column_sum(values, label_ids, segments):
    safe_ids = jnp.where(label_ids >= 0, label_ids, segments)
    totals = jnp.zeros((values.shape[0], segments), jnp.float32)
    return totals.at[:, safe_ids].add(values.astype(jnp.float32), mode="drop")


def halo_rows(field_rows, send_lists, move_fn):
    offsets = send_lists.shape[0]
    radius = (offsets - 1) // 2
    pieces = []
    for slot_id in range(offsets):
        picked = jnp.take(field_rows, send_lists[slot_id], axis=1)
        if slot_id != radius:
            picked = move_fn(picked, slot_id - radius)
        pieces.append(picked)
    return jnp.concatenate(pieces, axis=1)


def halo_back(row_grads, send_lists, row_total, move_fn):
    offsets, capacity = send_lists.shape
    radius = (offsets - 1) // 2
    totals = jnp.zeros((row_grads.shape[0], row_total), jnp.float32)
    for slot_id in range(offsets):
        portion = row_grads[:, slot_id * capacity : (slot_id + 1) * capacity]
        if slot_id != radius:
            portion = move_fn(portion, radius - slot_id)
        totals = totals.at[:, send_lists[slot_id]].add(portion)
    return totals


def edge_pre(sender_terms, recv_terms, features, sources, targets, w_edge):
    present = targets >= 0
    anchors = jnp.where(present, targets, 0)
    pre_act = (
        jnp.take(sender_terms, sources, axis=1)
        + jnp.take(recv_terms, anchors, axis=1)
        + contract(w_edge, features)
    )
    return (pre_act, present, anchors)


def norm_stats(out_part, full_width, moments_fn):
    first_sum, square_sum = moments_fn(
        (jnp.sum(out_part, axis=0), jnp.sum(out_part * out_part, axis=0))
    )
    average = first_sum / full_width
    variance = square_sum / full_width - average * average
    inverse = lax.rsqrt(variance + eps)
    return ((out_part - average[None, :]) * inverse[None, :], inverse)


def node_forward(
    latent, gathered, w_latent, w_gather, w_out, scale_gain, reduce_hidden, reduce_out, moments_fn
):
    pre_hidden = reduce_hidden(
        lambda row_start, row_count: contract(w_latent, latent) + contract(w_gather, gathered)
    )
    hidden = jax.nn.silu(pre_hidden).astype(jnp.bfloat16)
    out_part = reduce_out(lambda row_start, row_count: contract(w_out, hidden))
    normed, inverse = norm_stats(out_part, w_out.shape[1], moments_fn)
    updated = (latent.astype(jnp.float32) + normed * scale_gain[:, None]).astype(jnp.bfloat16)
    return (updated, pre_hidden, normed, inverse)


def norm_back(grad_in, normed, inverse, scale_gain, full_width, combine):
    scaled = grad_in * scale_gain[:, None]
    total_a, total_b = combine((jnp.sum(scaled, axis=0), jnp.sum(scaled * normed, axis=0)))
    result = (
        scaled - total_a[None, :] / full_width - normed * (total_b[None, :] / full_width)
    ) * inverse[None, :]
    return result.astype(jnp.bfloat16)


def edge_sums(d_gather, pre_act, present, anchors, sources, targets, segments, buffer_rows):
    d_edges = jnp.where(present[None, :], jnp.take(d_gather, anchors, axis=1), 0.0)
    d_pre = (d_edges * silu_grad(pre_act)).astype(jnp.bfloat16)
    return (column_sum(d_pre, targets, segments), column_sum(d_pre, sources, buffer_rows))


def edge_back(
    d_gather, pre_act, present, anchors, sources, targets, w_send, w_recv, segments, buffer_rows
):
    recv_sum, rows_sum = edge_sums(
        d_gather, pre_act, present, anchors, sources, targets, segments, buffer_rows
    )
    d_recv = expand(w_recv, recv_sum.astype(jnp.bfloat16))
    d_rows = expand(w_send, rows_sum.astype(jnp.bfloat16))
    return (d_recv, d_rows)


def split_channels(
    grid_in,
    w_grid,
    mesh_in,
    g2m_attr,
    g2m_send,
    g2m_src,
    g2m_dst,
    w_gs,
    w_gr,
    w_ge,
    w_nm,
    w_na,
    w_no,
    gain_enc,
    mesh_attr,
    mesh_send,
    mesh_src,
    mesh_dst,
    w_ms,
    w_mr,
    w_me,
    w_pm,
    w_pa,
    w_po,
    gain_proc,
    cotangent,
):
    full_width = w_gs.shape[0]
    chan_share = full_width // lax.axis_size("chan")
    grid_rows = grid_in.shape[1]
    mesh_rows = mesh_in.shape[1]
    grid_pre = contract(w_grid, grid_in)
    grid_lat = jax.nn.silu(grid_pre).astype(jnp.bfloat16)
    grid_full = lax.all_gather(grid_lat, "chan", axis=0, tiled=True)
    grid_buffer = halo_rows(
        grid_full, g2m_send, lambda payload, amount: from_behind(payload, "band", amount)
    )
    mesh_full = lax.all_gather(mesh_in, "chan", axis=0, tiled=True)
    enc_pre, enc_present, enc_anchors = edge_pre(
        contract(w_gs, grid_buffer), contract(w_gr, mesh_full), g2m_attr, g2m_src, g2m_dst, w_ge
    )
    enc_gather = column_sum(jax.nn.silu(enc_pre).astype(jnp.bfloat16), g2m_dst, mesh_rows).astype(
        jnp.bfloat16
    )
    mesh_mid, enc_hidden_pre, enc_normed, enc_inverse = node_forward(
        mesh_in,
        enc_gather,
        w_nm,
        w_na,
        w_no,
        gain_enc,
        lambda term_fn: lax.psum_scatter(
            term_fn(jnp.int32(0), chan_share * lax.axis_size("chan")).astype(jnp.bfloat16),
            "chan",
            scatter_dimension=0,
            tiled=True,
        ).astype(jnp.float32),
        lambda term_fn: lax.psum_scatter(
            term_fn(jnp.int32(0), chan_share * lax.axis_size("chan")).astype(jnp.bfloat16),
            "chan",
            scatter_dimension=0,
            tiled=True,
        ).astype(jnp.float32),
        lambda payload: lax.psum(payload, "chan"),
    )
    mid_full = lax.all_gather(mesh_mid, "chan", axis=0, tiled=True)
    mesh_buffer = halo_rows(
        mid_full, mesh_send, lambda payload, amount: from_behind(payload, "band", amount)
    )
    proc_pre, proc_present, proc_anchors = edge_pre(
        contract(w_ms, mesh_buffer), contract(w_mr, mid_full), mesh_attr, mesh_src, mesh_dst, w_me
    )
    proc_gather = column_sum(
        jax.nn.silu(proc_pre).astype(jnp.bfloat16), mesh_dst, mesh_rows
    ).astype(jnp.bfloat16)
    mesh_out, proc_hidden_pre, proc_normed, proc_inverse = node_forward(
        mesh_mid,
        proc_gather,
        w_pm,
        w_pa,
        w_po,
        gain_proc,
        lambda term_fn: lax.psum_scatter(
            term_fn(jnp.int32(0), chan_share * lax.axis_size("chan")).astype(jnp.bfloat16),
            "chan",
            scatter_dimension=0,
            tiled=True,
        ).astype(jnp.float32),
        lambda term_fn: lax.psum_scatter(
            term_fn(jnp.int32(0), chan_share * lax.axis_size("chan")).astype(jnp.bfloat16),
            "chan",
            scatter_dimension=0,
            tiled=True,
        ).astype(jnp.float32),
        lambda payload: lax.psum(payload, "chan"),
    )
    top_grad = cotangent.astype(jnp.float32)
    d_out = norm_back(
        top_grad,
        proc_normed,
        proc_inverse,
        gain_proc,
        full_width,
        lambda payload: lax.psum(payload, "chan"),
    )
    d_hidden = expand(w_po, lax.all_gather(d_out, "chan", axis=0, tiled=True))
    d_pre = (d_hidden * silu_grad(proc_hidden_pre)).astype(jnp.bfloat16)
    d_pre_full = lax.all_gather(d_pre, "chan", axis=0, tiled=True)
    d_mid = top_grad + expand(w_pm, d_pre_full)
    d_recv, d_rows = edge_back(
        expand(w_pa, d_pre_full),
        proc_pre,
        proc_present,
        proc_anchors,
        mesh_src,
        mesh_dst,
        w_ms,
        w_mr,
        mesh_rows,
        mesh_buffer.shape[1],
    )
    back_rows = halo_back(
        d_rows,
        mesh_send,
        mesh_rows,
        lambda payload, amount: from_behind(payload.astype(jnp.bfloat16), "band", amount).astype(
            payload.dtype
        ),
    )
    d_mid = d_mid + lax.psum_scatter(
        (d_recv + back_rows).astype(jnp.bfloat16), "chan", scatter_dimension=0, tiled=True
    ).astype(jnp.float32)
    d_out = norm_back(
        d_mid,
        enc_normed,
        enc_inverse,
        gain_enc,
        full_width,
        lambda payload: lax.psum(payload, "chan"),
    )
    d_hidden = expand(w_no, lax.all_gather(d_out, "chan", axis=0, tiled=True))
    d_pre = (d_hidden * silu_grad(enc_hidden_pre)).astype(jnp.bfloat16)
    d_pre_full = lax.all_gather(d_pre, "chan", axis=0, tiled=True)
    mesh_grad = d_mid + expand(w_nm, d_pre_full)
    d_recv, d_rows = edge_back(
        expand(w_na, d_pre_full),
        enc_pre,
        enc_present,
        enc_anchors,
        g2m_src,
        g2m_dst,
        w_gs,
        w_gr,
        mesh_rows,
        grid_buffer.shape[1],
    )
    back_rows = halo_back(
        d_rows,
        g2m_send,
        grid_rows,
        lambda payload, amount: from_behind(payload.astype(jnp.bfloat16), "band", amount).astype(
            payload.dtype
        ),
    )
    grid_grad, recv_part = (
        lax.psum_scatter(
            back_rows.astype(jnp.bfloat16), "chan", scatter_dimension=0, tiled=True
        ).astype(jnp.float32),
        lax.psum_scatter(
            d_recv.astype(jnp.bfloat16), "chan", scatter_dimension=0, tiled=True
        ).astype(jnp.float32),
    )
    mesh_grad = mesh_grad + recv_part
    return (mesh_out, mesh_grad, grid_grad, grid_pre)


def local(
    grid_in,
    w_grid,
    mesh_in,
    g2m_attr,
    g2m_send,
    g2m_src,
    g2m_dst,
    w_gs,
    w_gr,
    w_ge,
    w_nm,
    w_na,
    w_no,
    gain_enc,
    mesh_attr,
    mesh_send,
    mesh_src,
    mesh_dst,
    w_ms,
    w_mr,
    w_me,
    w_pm,
    w_pa,
    w_po,
    gain_proc,
    cotangent,
):
    mesh_out, mesh_grad, grid_grad, grid_pre = split_channels(
        grid_in,
        w_grid,
        mesh_in,
        g2m_attr,
        g2m_send,
        g2m_src,
        g2m_dst,
        w_gs,
        w_gr,
        w_ge,
        w_nm,
        w_na,
        w_no,
        gain_enc,
        mesh_attr,
        mesh_send,
        mesh_src,
        mesh_dst,
        w_ms,
        w_mr,
        w_me,
        w_pm,
        w_pa,
        w_po,
        gain_proc,
        cotangent,
    )
    d_grid_pre = (grid_grad * silu_grad(grid_pre)).astype(jnp.bfloat16)
    w_part = lax.dot_general(
        grid_in, d_grid_pre, (((1,), (1,)), ((), ())), preferred_element_type=jnp.float32
    )
    grad_scale = float(grid_in.shape[1] * lax.axis_size("band")) ** (-0.5)
    w_grid_grad = lax.psum(w_part, "band") * grad_scale
    return (mesh_out, mesh_grad, w_grid_grad)


def solution(mesh):
    return jax.shard_map(
        local,
        mesh=mesh,
        in_specs=(
            P(None, "band"),
            P(None, "chan"),
            P("chan", "band"),
            P(None, "band"),
            P("band", None),
            P("band"),
            P("band"),
            P(None, "chan"),
            P(None, "chan"),
            P(None, "chan"),
            P("chan", None),
            P("chan", None),
            P("chan", None),
            P("chan"),
            P(None, "band"),
            P("band", None),
            P("band"),
            P("band"),
            P(None, "chan"),
            P(None, "chan"),
            P(None, "chan"),
            P("chan", None),
            P("chan", None),
            P("chan", None),
            P("chan"),
            P("chan", "band"),
        ),
        out_specs=(P("chan", "band"), P("chan", "band"), P(None, "chan")),
        check_vma=False,
    )
```

profile of v0, /device:TPU:1, one launch (start us, length us, event | category | flops | bytes accessed | tf_op | source)
XLA Modules:
  0.0 1060.2 jit_solution(8760707103122948455)
XLA Ops:
  13.0 12.3 %all_gather.22 = bf16[512,512]{1,0:T(8,128)(2,1)S(1)} all-gather(bf16[128,512]{1,0:T(8,128)(2,1)S(1)} %copy-done.8), channel_id=1, replica_groups=mesh['band'=64,'chan'=4] {'chan'}, dimensions={0}, use_global_device_ids=true | all-gather | bytes 655360 | tf_op jit(solution)/shard_map/all_gather | solution.py:158
  25.7 27.7 %gather_fusion.7 = f32[8192,128]{1,0:T(8,128)} fusion(f32[128,512]{0,1:T(8,128)S(1)} %fusion.119, s32[8192]{0:T(1024)S(1)} %get-tuple-element.43), kind=kCustom, calls=%fused_computation.1.clone | custom fusion | bytes 8421376 | tf_op jit(solution)/shard_map/jit(_take)/gather | solution.py:65
  110.4 27.7 %gather_fusion = f32[8192,128]{1,0:T(8,128)} fusion(f32[128,2560]{0,1:T(8,128)S(1)} %convolution_bitcast_fusion.1, s32[8192]{0:T(1024)S(1)} %get-tuple-element.40), kind=kCustom, calls=%fused_computation.14 | custom fusion | bytes 8421376 | tf_op jit(solution)/shard_map/jit(_take)/gather | solution.py:64
  158.9 54.2 %scatter_custom_fusion = f32[128,512]{0,1:T(8,128)S(1)} fusion(s32[8192]{0:T(1024)} %get-tuple-element.44, f32[8192,128]{1,0:T(8,128)} %copy.95, f32[]{:T(128)} %constant.54.clone.1), kind=kCustom, calls=%fused_computation.194 | custom fusion | flops 1048576 | bytes 262656 | tf_op jit(solution)/shard_map/scatter-add | solution.py:33
  215.0 24.2 %reduce-scatter.16.cloned.1.call-done = bf16[128,512]{1,0:T(8,128)(2,1)} async-done(((bf16[512,512]{1,0:T(8,128)(2,1)}), bf16[128,512]{1,0:T(8,128)(2,1)}) %reduce-scatter.16.cloned.1.call-update) | async-done | bytes 131088 | tf_op jit(solution)/shard_map/reduce_scatter | solution.py:172
  243.5 22.0 %reduce-scatter.22.cloned.1.call-done = bf16[128,512]{1,0:T(8,128)(2,1)} async-done(((bf16[512,512]{1,0:T(8,128)(2,1)}), bf16[128,512]{1,0:T(8,128)(2,1)}) %reduce-scatter.22.cloned.1.call-update) | async-done | bytes 131088 | tf_op jit(solution)/shard_map/reduce_scatter | solution.py:178
  285.0 14.1 %gather_fusion.13 = f32[4096,128]{1,0:T(8,128)} fusion(f32[128,512]{0,1:T(8,128)S(1)} %convolution_bitcast_fusion.12, s32[4096]{0:T(1024)S(1)} %get-tuple-element.54), kind=kCustom, calls=%fused_computation.3.clone | custom fusion | bytes 4210688 | tf_op jit(solution)/shard_map/jit(_take)/gather | solution.py:65
  333.9 14.1 %gather_fusion.1 = f32[4096,128]{1,0:T(8,128)} fusion(f32[128,1280]{0,1:T(8,128)S(1)} %convolution_bitcast_fusion.3, s32[4096]{0:T(1024)S(1)} %get-tuple-element.51), kind=kCustom, calls=%fused_computation.15 | custom fusion | bytes 4210688 | tf_op jit(solution)/shard_map/jit(_take)/gather | solution.py:64
  358.5 26.8 %scatter_custom_fusion.1 = f32[128,512]{0,1:T(8,128)S(1)} fusion(s32[4096]{0:T(1024)} %get-tuple-element.55, f32[4096,128]{1,0:T(8,128)} %copy.105, f32[]{:T(128)} %constant.54.clone.1), kind=kCustom, calls=%fused_computation.192 | custom fusion | flops 524288 | bytes 262656 | tf_op jit(solution)/shard_map/scatter-add | solution.py:33
  387.8 23.9 %reduce-scatter.18.cloned.1.call-done = bf16[128,512]{1,0:T(8,128)(2,1)} async-done(((bf16[512,512]{1,0:T(8,128)(2,1)}), bf16[128,512]{1,0:T(8,128)(2,1)}) %reduce-scatter.18.cloned.1.call-update) | async-done | bytes 131088 | tf_op jit(solution)/shard_map/reduce_scatter | solution.py:203
  416.0 23.8 %reduce-scatter.24.cloned.1.call-done = bf16[128,512]{1,0:T(8,128)(2,1)} async-done(((bf16[512,512]{1,0:T(8,128)(2,1)}), bf16[128,512]{1,0:T(8,128)(2,1)}) %reduce-scatter.24.cloned.1.call-update) | async-done | bytes 131088 | tf_op jit(solution)/shard_map/reduce_scatter | solution.py:209
  481.1 14.2 %gather_fusion.14 = f32[4096,128]{1,0:T(8,128)} fusion(f32[128,512]{0,1:T(8,128)S(1)} %convolution_bitcast_fusion.11, s32[4096]{0:T(1024)S(1)} %get-tuple-element.54), kind=kCustom, calls=%fused_computation.13.clone | custom fusion | bytes 4210688 | tf_op jit(solution)/shard_map/jit(_take)/gather | solution.py:104
  504.9 22.8 %scatter_custom_fusion.3 = f32[128,1280]{0,1:T(8,128)S(1)} fusion(s32[4096]{0:T(1024)} %get-tuple-element.50, f32[4096,128]{1,0:T(8,128)} %copy.111, f32[]{:T(128)} %constant.54.clone.1), kind=kCustom, calls=%fused_computation.140 | custom fusion | flops 524288 | bytes 655872 | tf_op jit(solution)/shard_map/scatter-add | solution.py:33
  534.6 15.3 %collective-permute-start.9 = (bf16[512,256]{0,1:T(8,128)(2,1)}, bf16[512,256]{0,1:T(8,128)(2,1)S(1)}, u32[]{:S(2)}, u32[]{:S(2)}) collective-permute-start(bf16[512,256]{0,1:T(8,128)(2,1)} %get-tuple-element.35), channel_id=1, source_target_pairs={{0,4},{4,8},{8,12},{12,16},{16,20},{20,24},{24,28},{28,32},{32,36}... | collective-permute-start | bytes 786440 | tf_op jit(solution)/shard_map/ppermute | solution.py:12
  553.3 26.8 %scatter_custom_fusion.2 = f32[128,512]{0,1:T(8,128)S(1)} fusion(s32[4096]{0:T(1024)} %get-tuple-element.55, f32[4096,128]{1,0:T(8,128)} %copy.111, f32[]{:T(128)} %constant.54.clone.1), kind=kCustom, calls=%fused_computation.190 | custom fusion | flops 524288 | bytes 262656 | tf_op jit(solution)/shard_map/scatter-add | solution.py:33
  595.3 24.4 %reduce-scatter.26.cloned.1.call-done = bf16[128,512]{1,0:T(8,128)(2,1)} async-done(((bf16[512,512]{1,0:T(8,128)(2,1)}), bf16[128,512]{1,0:T(8,128)(2,1)}) %reduce-scatter.26.cloned.1.call-update) | async-done | bytes 131088 | tf_op jit(solution)/shard_map/reduce_scatter | solution.py:250
  627.9 10.3 all_gather.26
  638.4 10.7 %all_gather.27 = bf16[512,512]{1,0:T(8,128)(2,1)S(1)} all-gather(bf16[128,512]{1,0:T(8,128)(2,1)S(1)} %fusion.18), channel_id=1, replica_groups=mesh['band'=64,'chan'=4] {'chan'}, dimensions={0}, use_global_device_ids=true | all-gather | bytes 655360 | tf_op jit(solution)/shard_map/all_gather | solution.py:263
  650.2 27.9 %gather_fusion.15 = f32[8192,128]{1,0:T(8,128)} fusion(f32[128,512]{0,1:T(8,128)S(1)} %convolution_bitcast_fusion.10, s32[8192]{0:T(1024)S(1)} %get-tuple-element.43), kind=kCustom, calls=%fused_computation.8.clone | custom fusion | bytes 8421376 | tf_op jit(solution)/shard_map/jit(_take)/gather | solution.py:104
  696.4 44.6 %scatter_custom_fusion.10 = f32[128,2560]{0,1:T(8,128)S(1)} fusion(s32[8192]{0:T(1024)} %get-tuple-element.39, f32[8192,128]{1,0:T(8,128)} %copy.117, f32[]{:T(128)} %constant.54.clone.1), kind=kCustom, calls=%fused_computation.99 | custom fusion | flops 1048576 | bytes 1311232 | tf_op jit(solution)/shard_map/scatter-add | solution.py:33
  748.7 12.7 %collective-permute-start.13 = (bf16[512,512]{0,1:T(8,128)(2,1)}, bf16[512,512]{0,1:T(8,128)(2,1)}, u32[]{:S(2)}, u32[]{:S(2)}) collective-permute-start(bf16[512,512]{0,1:T(8,128)(2,1)} %get-tuple-element.31), channel_id=1, source_target_pairs={{0,4},{4,8},{8,12},{12,16},{16,20},{20,24},{24,28},{28,32},{32,36}... | collective-permute-start | bytes 1572872 | tf_op jit(solution)/shard_map/ppermute | solution.py:12
  792.0 54.2 %scatter_custom_fusion.9 = f32[128,512]{0,1:T(8,128)S(1)} fusion(s32[8192]{0:T(1024)} %get-tuple-element.44, f32[8192,128]{1,0:T(8,128)} %copy.117, f32[]{:T(128)} %constant.54.clone.1), kind=kCustom, calls=%fused_computation.188 | custom fusion | flops 1048576 | bytes 262656 | tf_op jit(solution)/shard_map/scatter-add | solution.py:33
  849.9 22.2 %reduce-scatter.28.cloned.1.call-done = bf16[128,512]{1,0:T(8,128)(2,1)} async-done(((bf16[512,512]{1,0:T(8,128)(2,1)}), bf16[128,512]{1,0:T(8,128)(2,1)}) %reduce-scatter.28.cloned.1.call-update) | async-done | bytes 131088 | tf_op jit(solution)/shard_map/reduce_scatter | solution.py:289
  874.0 177.6 %all-reduce.6.cloned.1.call-done = f32[474,128]{1,0:T(8,128)} async-done(((f32[474,128]{1,0:T(8,128)}), f32[474,128]{1,0:T(8,128)}) %all-reduce.6.cloned.1.call-update) | async-done | bytes 242704 | tf_op jit(solution)/shard_map/psum | solution.py:358
  (304 shorter events, 310.3 us)
Async XLA Ops:
  7.2 54.6 %all-gather.2.cloned.1.call-start = ((), (), s32[]{:S(2)}) async-start(), calls=%async_computation.7 | async-start | bytes 1310720 | tf_op jit(solution)/shard_map/all_gather | solution.py:154
  10.5 228.7 %reduce-scatter.16.cloned.1.call-start = ((), (), s32[]{:S(2)}) async-start(), calls=%async_computation.8 | async-start | bytes 655360 | tf_op jit(solution)/shard_map/reduce_scatter | solution.py:172
  68.0 30.6 %collective-permute-start = (bf16[512,512]{0,1:T(8,128)(2,1)}, bf16[512,512]{0,1:T(8,128)(2,1)}, u32[]{:S(2)}, u32[]{:S(2)}) collective-permute-start(bf16[512,512]{0,1:T(8,128)(2,1)} %select_bitcast_fusion.3), channel_id=1, source_target_pairs={{8,0},{12,4},{16,8},{20,12},{24,16},{28,20},{32,24},{36,28},{40,32... | collective-permute-start | bytes 1572872 | tf_op jit(solution)/shard_map/ppermute | solution.py:12
  73.9 25.8 %collective-permute-start.1 = (bf16[512,512]{0,1:T(8,128)(2,1)}, bf16[512,512]{0,1:T(8,128)(2,1)}, u32[]{:S(2)}, u32[]{:S(2)}) collective-permute-start(bf16[512,512]{0,1:T(8,128)(2,1)} %select_bitcast_fusion.2), channel_id=1, source_target_pairs={{4,0},{8,4},{12,8},{16,12},{20,16},{24,20},{28,24},{32,28},{36,32}... | collective-permute-start | bytes 1572872 | tf_op jit(solution)/shard_map/ppermute | solution.py:12
  84.8 16.3 %collective-permute-start.2 = (bf16[512,512]{0,1:T(8,128)(2,1)}, bf16[512,512]{0,1:T(8,128)(2,1)}, u32[]{:S(2)}, u32[]{:S(2)}) collective-permute-start(bf16[512,512]{0,1:T(8,128)(2,1)} %select_bitcast_fusion.1), channel_id=1, source_target_pairs={{0,4},{4,8},{8,12},{12,16},{16,20},{20,24},{24,28},{28,32},{32,36}... | collective-permute-start | bytes 1572872 | tf_op jit(solution)/shard_map/ppermute | solution.py:12
  96.3 13.2 %collective-permute-start.3 = (bf16[512,512]{0,1:T(8,128)(2,1)}, bf16[512,512]{0,1:T(8,128)(2,1)S(1)}, u32[]{:S(2)}, u32[]{:S(2)}) collective-permute-start(bf16[512,512]{0,1:T(8,128)(2,1)} %select_bitcast_fusion), channel_id=1, source_target_pairs={{0,8},{4,12},{8,16},{12,20},{16,24},{20,28},{24,32},{28,36},{32,40... | collective-permute-start | bytes 1572872 | tf_op jit(solution)/shard_map/ppermute | solution.py:12
  214.4 51.1 %reduce-scatter.22.cloned.1.call-start = ((), (), s32[]{:S(2)}) async-start(), calls=%async_computation.12 | async-start | bytes 655360 | tf_op jit(solution)/shard_map/reduce_scatter | solution.py:178
  241.5 170.2 %reduce-scatter.18.cloned.1.call-start = ((), (), s32[]{:S(2)}) async-start(), calls=%async_computation.9 | async-start | bytes 655360 | tf_op jit(solution)/shard_map/reduce_scatter | solution.py:203
  303.3 25.9 %collective-permute-start.4 = (bf16[512,256]{0,1:T(8,128)(2,1)S(1)}, bf16[512,256]{0,1:T(8,128)(2,1)}, u32[]{:S(2)}, u32[]{:S(2)}) collective-permute-start(bf16[512,256]{0,1:T(8,128)(2,1)S(1)} %select_bitcast_fusion.7), channel_id=1, source_target_pairs={{8,0},{12,4},{16,8},{20,12},{24,16},{28,20},{32,24},{36,28},{40,32... | collective-permute-start | bytes 786440 | tf_op jit(solution)/shard_map/ppermute | solution.py:12
  306.6 23.6 %collective-permute-start.5 = (bf16[512,256]{0,1:T(8,128)(2,1)}, bf16[512,256]{0,1:T(8,128)(2,1)}, u32[]{:S(2)}, u32[]{:S(2)}) collective-permute-start(bf16[512,256]{0,1:T(8,128)(2,1)} %select_bitcast_fusion.6), channel_id=1, source_target_pairs={{4,0},{8,4},{12,8},{16,12},{20,16},{24,20},{28,24},{32,28},{36,32}... | collective-permute-start | bytes 786440 | tf_op jit(solution)/shard_map/ppermute | solution.py:12
  318.7 12.6 %collective-permute-start.6 = (bf16[512,256]{0,1:T(8,128)(2,1)}, bf16[512,256]{0,1:T(8,128)(2,1)}, u32[]{:S(2)}, u32[]{:S(2)}) collective-permute-start(bf16[512,256]{0,1:T(8,128)(2,1)} %select_bitcast_fusion.5), channel_id=1, source_target_pairs={{0,4},{4,8},{8,12},{12,16},{16,20},{20,24},{24,28},{28,32},{32,36}... | collective-permute-start | bytes 786440 | tf_op jit(solution)/shard_map/ppermute | solution.py:12
  387.8 52.0 %reduce-scatter.24.cloned.1.call-start = ((), (), s32[]{:S(2)}) async-start(), calls=%async_computation.13 | async-start | bytes 655360 | tf_op jit(solution)/shard_map/reduce_scatter | solution.py:209
  415.9 203.8 %reduce-scatter.26.cloned.1.call-start = ((), (), s32[]{:S(2)}) async-start(), calls=%async_computation.14 | async-start | bytes 655360 | tf_op jit(solution)/shard_map/reduce_scatter | solution.py:250
  530.7 49.7 %collective-permute-start.8 = (bf16[512,256]{0,1:T(8,128)(2,1)}, bf16[512,256]{0,1:T(8,128)(2,1)}, u32[]{:S(2)}, u32[]{:S(2)}) collective-permute-start(bf16[512,256]{0,1:T(8,128)(2,1)} %get-tuple-element.36), channel_id=1, source_target_pairs={{0,8},{4,12},{8,16},{12,20},{16,24},{20,28},{24,32},{28,36},{32,40... | collective-permute-start | bytes 786440 | tf_op jit(solution)/shard_map/ppermute | solution.py:12
  534.6 48.8 %collective-permute-start.9 = (bf16[512,256]{0,1:T(8,128)(2,1)}, bf16[512,256]{0,1:T(8,128)(2,1)S(1)}, u32[]{:S(2)}, u32[]{:S(2)}) collective-permute-start(bf16[512,256]{0,1:T(8,128)(2,1)} %get-tuple-element.35), channel_id=1, source_target_pairs={{0,4},{4,8},{8,12},{12,16},{16,20},{20,24},{24,28},{28,32},{32,36}... | collective-permute-start | bytes 786440 | tf_op jit(solution)/shard_map/ppermute | solution.py:12
  549.9 39.1 %collective-permute-start.10 = (bf16[512,256]{0,1:T(8,128)(2,1)}, bf16[512,256]{0,1:T(8,128)(2,1)S(1)}, u32[]{:S(2)}, u32[]{:S(2)}) collective-permute-start(bf16[512,256]{0,1:T(8,128)(2,1)} %get-tuple-element.34), channel_id=1, source_target_pairs={{4,0},{8,4},{12,8},{16,12},{20,16},{24,20},{28,24},{32,28},{36,32}... | collective-permute-start | bytes 786440 | tf_op jit(solution)/shard_map/ppermute | solution.py:12
  551.8 39.7 %collective-permute-start.11 = (bf16[512,256]{0,1:T(8,128)(2,1)}, bf16[512,256]{0,1:T(8,128)(2,1)S(1)}, u32[]{:S(2)}, u32[]{:S(2)}) collective-permute-start(bf16[512,256]{0,1:T(8,128)(2,1)} %get-tuple-element.33), channel_id=1, source_target_pairs={{8,0},{12,4},{16,8},{20,12},{24,16},{28,20},{32,24},{36,28},{40,32... | collective-permute-start | bytes 786440 | tf_op jit(solution)/shard_map/ppermute | solution.py:12
  595.3 252.4 %reduce-scatter.20.cloned.1.call-start = ((), (), s32[]{:S(2)}) async-start(), calls=%async_computation.10 | async-start | bytes 1310720 | tf_op jit(solution)/shard_map/reduce_scatter | solution.py:286
  745.5 19.2 %collective-permute-start.12 = (bf16[512,512]{0,1:T(8,128)(2,1)S(1)}, bf16[512,512]{0,1:T(8,128)(2,1)S(1)}, u32[]{:S(2)}, u32[]{:S(2)}) collective-permute-start(bf16[512,512]{0,1:T(8,128)(2,1)S(1)} %get-tuple-element.32), channel_id=1, source_target_pairs={{0,8},{4,12},{8,16},{12,20},{16,24},{20,28},{24,32},{28,36},{32,40... | collective-permute-start | bytes 1572872 | tf_op jit(solution)/shard_map/ppermute | solution.py:12
  748.7 21.6 %collective-permute-start.13 = (bf16[512,512]{0,1:T(8,128)(2,1)}, bf16[512,512]{0,1:T(8,128)(2,1)}, u32[]{:S(2)}, u32[]{:S(2)}) collective-permute-start(bf16[512,512]{0,1:T(8,128)(2,1)} %get-tuple-element.31), channel_id=1, source_target_pairs={{0,4},{4,8},{8,12},{12,16},{16,20},{20,24},{24,28},{28,32},{32,36}... | collective-permute-start | bytes 1572872 | tf_op jit(solution)/shard_map/ppermute | solution.py:12
  761.4 19.2 %collective-permute-start.14 = (bf16[512,512]{0,1:T(8,128)(2,1)}, bf16[512,512]{0,1:T(8,128)(2,1)}, u32[]{:S(2)}, u32[]{:S(2)}) collective-permute-start(bf16[512,512]{0,1:T(8,128)(2,1)} %get-tuple-element.30), channel_id=1, source_target_pairs={{4,0},{8,4},{12,8},{16,12},{20,16},{24,20},{28,24},{32,28},{36,32}... | collective-permute-start | bytes 1572872 | tf_op jit(solution)/shard_map/ppermute | solution.py:12
  763.4 22.2 %collective-permute-start.15 = (bf16[512,512]{0,1:T(8,128)(2,1)}, bf16[512,512]{0,1:T(8,128)(2,1)}, u32[]{:S(2)}, u32[]{:S(2)}) collective-permute-start(bf16[512,512]{0,1:T(8,128)(2,1)} %get-tuple-element.29), channel_id=1, source_target_pairs={{8,0},{12,4},{16,8},{20,12},{24,16},{28,20},{32,24},{36,28},{40,32... | collective-permute-start | bytes 1572872 | tf_op jit(solution)/shard_map/ppermute | solution.py:12
  791.9 80.2 %reduce-scatter.28.cloned.1.call-start = ((), (), s32[]{:S(2)}) async-start(), calls=%async_computation.15 | async-start | bytes 655360 | tf_op jit(solution)/shard_map/reduce_scatter | solution.py:289
  847.6 204.0 %all-reduce.6.cloned.1.call-start = ((), (), s32[]{:S(2)}) async-start(), calls=%async_computation.11 | async-start | bytes 491520 | tf_op jit(solution)/shard_map/psum | solution.py:358
  (57 other events, 1372.6 us)
Sparse Core Ops, SparseCore 0:
  10.6 29.3 all-gather.1
  214.5 24.6 reduce-scatter.15
  241.8 23.7 reduce-scatter.21
  387.9 23.7 reduce-scatter.17
  416.0 23.7 reduce-scatter.23
  595.4 24.2 reduce-scatter.25
  792.0 29.4 reduce-scatter.19
  847.7 24.4 reduce-scatter.27
  876.6 174.9 all-reduce.5
where the time goes:
time: 1070 us; the launch traced here: 1060 us
  waiting for transfers between devices  327 us (31%)
  other arithmetic  309 us (29%)
  local copies, waits for them, and re-layouts  211 us (20%)
  blocking collectives  90.7 us (8%)
  starting transfers between devices  74.2 us (7%)
  matrix products  33.1 us (3%)
  between operations  15.4 us (1%)
    scatter-add x6, other arithmetic, column_sum(): return totals.at[:, safe_ids].add(values.astype(jnp.float32), mode='drop')  229 us
    psum x1, waiting for transfers between devices, local(): w_grid_grad = lax.psum(w_part, 'band') * grad_scale  178 us
    reduce_scatter x4, waiting for transfers between devices, split_channels(): lax.psum_scatter(term_fn(jnp.int32(0), chan_share * lax.axis_size('chan')...  93.9 us
    ppermute x16, starting transfers between devices, from_behind(): return lax.ppermute(block, axis, route)  73.9 us
    gather x4, local copies, waits for them, and re-layouts, edge_sums(): jnp.take(d_gather, anchors, axis=1)  50.6 us
    gather x4, local copies, waits for them, and re-layouts, edge_pre(): jnp.take(recv_terms, anchors, axis=1)  50.5 us
    gather x4, local copies, waits for them, and re-layouts, edge_pre(): jnp.take(sender_terms, sources, axis=1)  50.4 us
    scatter-add x10, other arithmetic, halo_back(): totals = totals.at[:, send_lists[slot_id]].add(portion)  38.3 us
  transfers between devices with their start and end apart: 25, of which 10 were waited for; matrix products, arithmetic and copies ran while one was open for 18% of the time, Pallas kernels for 0%

commit v1 on v0

v1 whole, which is shorter than its diff:
```python
import functools

import jax
import jax.numpy as jnp
from jax import lax
from jax.experimental import pallas as pl
from jax.experimental.pallas import tpu as pltpu
from jax.sharding import PartitionSpec as P

eps = 1e-05
bf16 = jnp.bfloat16
f32 = jnp.float32
MESH = pl.DeviceIdType.MESH
SEMS = 192
INPUTS = (
    *("grid_in", "w_grid", "mesh_in", "g2m_attr", "g2m_send", "g2m_src", "g2m_dst"),
    *("w_gs", "w_gr", "w_ge", "w_nm", "w_na", "w_no", "gain_enc"),
    *("mesh_attr", "mesh_send", "mesh_src", "mesh_dst"),
    *("w_ms", "w_mr", "w_me", "w_pm", "w_pa", "w_po", "gain_proc", "cotangent"),
)


def dot(a, b):
    return jnp.dot(a, b, preferred_element_type=f32)


def dot_nt(a, b):
    return lax.dot_general(a, b, (((1,), (1,)), ((), ())), preferred_element_type=f32)


def flip(x):
    return jnp.transpose(x.astype(f32))


def sigmoid(v):
    return 0.5 + 0.5 * jnp.tanh(0.5 * v)


def one_hot(ids, count):
    rows = lax.broadcasted_iota(jnp.int16, (count, ids.shape[1]), 0)
    return jnp.where(rows == ids.astype(jnp.int16), jnp.ones((), bf16), jnp.zeros((), bf16))


def slots_of(ids, capacity, slots):
    slot = jnp.zeros_like(ids)
    for j in range(1, slots):
        slot = slot + (ids >= j * capacity).astype(jnp.int32)
    return slot, ids - slot * capacity


def halves_of(ids, half):
    upper = ids >= half
    return upper, jnp.where(upper, ids - half, ids)


def two_rows(x):
    half = x.shape[1] // 2
    return jnp.concatenate([x[:, :half], x[:, half:]], axis=0)


def norm(out):
    width = out.shape[1]
    mean = jnp.sum(out, axis=1, keepdims=True) / width
    var = jnp.sum(out * out, axis=1, keepdims=True) / width - mean * mean
    inverse = lax.rsqrt(var + eps)
    return (out - mean) * inverse, inverse


def norm_back(grad, normed, inverse, gain):
    width = grad.shape[1]
    u = grad * gain
    a = jnp.sum(u, axis=1, keepdims=True) / width
    b = jnp.sum(u * normed, axis=1, keepdims=True) / width
    return ((u - a - normed * b) * inverse).astype(bf16)


def kernel(
    nband, nchan, inner, scale,
    grid_hbm, w_grid_hbm, mesh_in, g2m_attr_hbm, g2m_send_hbm, g2m_src_hbm, g2m_dst_hbm,
    w_gs_hbm, w_gr_hbm, w_ge_hbm, w_nm, w_na, w_no, gain_enc_hbm,
    mesh_attr_hbm, mesh_send_hbm, mesh_src_hbm, mesh_dst_hbm,
    w_ms, w_mr, w_me_hbm, w_pm, w_pa, w_po, gain_proc_hbm, cotangent,
    mesh_out, mesh_grad, w_grid_grad,
    grid_in, w_grid, g2m_attr, g2m_send, g2m_src, g2m_dst, w_gs, w_gr, w_ge, gain_enc,
    mesh_attr, mesh_send, mesh_src, mesh_dst, w_me, gain_proc,
    gpad, wg_pad, wg_t, we_pad, attr_g, attr_m,
    mesh_full, gains, cot_rows,
    f_nm, f_na, f_no, f_pm, f_pa, f_po, f_gs, f_gr, f_ms, f_mr,
    sgrid, s_grid, halo_out, table, edge_grad, edge_back,
    acc, nbuf, enc_g,
    s_out, r_out, s_in, r_in, mid_s, m_halo_out, m_table, m_edge_grad, m_edge_back, m_nbuf, proc_g,
    mo_out, mo_in, dg_out, dg_in, rows_acc, m_back_out, m_back_in, mr_out, mr_in, h_out, h_in,
    de_out, de_in, g_rows_acc, g_back_out, g_back_in, er_out, er_in, mg_out, mg_in,
    dgrid_out, dgrid_in, dpre_out, dpre_in,
    part, rs1, mine, rs2, last, total,
    ssem, rsem, lsem,
):
    d, c = lax.axis_index("band"), lax.axis_index("chan")
    width, cb = w_gs.shape
    fin, grid_dev = grid_in.shape
    mesh_dev = mesh_in.shape[1]
    nb = mesh_dev // nchan
    gb = grid_dev // nchan
    half = mesh_dev // 2
    offs, cap = g2m_send.shape
    radius = offs // 2
    ea = w_ge.shape[0]
    count = [0]
    local_count = [0]
    started = []

    def at(index, size):
        return pl.ds(pl.multiple_of(index * size, size), size)

    def fetch_local(src, dst):
        copy = pltpu.make_async_copy(src, dst, lsem.at[local_count[0]])
        local_count[0] += 1
        copy.start()
        return copy

    def remote(src, dst, target):
        i = count[0]
        count[0] += 1
        copy = pltpu.make_async_remote_copy(
            src_ref=src, dst_ref=dst, send_sem=ssem.at[i], recv_sem=rsem.at[i],
            device_id=target, device_id_type=MESH,
        )
        copy.start()
        started.append(copy)
        return copy

    def sent(copies):
        for copy in copies:
            copy.wait_send()
            started[:] = [other for other in started if other is not copy]

    def arrive(copies):
        for copy in copies:
            copy.wait_recv()

    own_w_grid = fetch_local(w_grid_hbm, w_grid)
    own_w_gs = fetch_local(w_gs_hbm, w_gs)
    own_grid = fetch_local(grid_hbm, grid_in)
    own_mesh = fetch_local(mesh_in, mesh_full.at[at(c, cb), :])
    own_rest = [
        fetch_local(src, dst)
        for src, dst in (
            (g2m_send_hbm, g2m_send), (w_gr_hbm, w_gr), (w_ge_hbm, w_ge), (g2m_attr_hbm, g2m_attr),
            (g2m_src_hbm, g2m_src), (g2m_dst_hbm, g2m_dst), (gain_enc_hbm, gain_enc), (gain_proc_hbm, gain_proc),
            (mesh_attr_hbm, mesh_attr), (mesh_send_hbm, mesh_send), (mesh_src_hbm, mesh_src),
            (mesh_dst_hbm, mesh_dst), (w_me_hbm, w_me), (cotangent.at[:, at(c, nb)], cot_rows.at[at(c, cb), :]),
        )
    ]

    chan_peers = [lax.rem(c + k, nchan) for k in range(1, nchan)]

    def band_at(offset):
        return lax.rem(d + offset + nband, nband)

    near = [band_at(o) for o in range(-radius, radius + 1) if o != 0]
    group, place = d // inner, lax.rem(d, inner)
    inner_peers = [group * inner + lax.rem(place + k, inner) for k in range(1, inner)]
    outer = nband // inner
    outer_peers = [lax.rem(group + k, outer) * inner + place for k in range(1, outer)]
    barrier = pltpu.get_barrier_semaphore()
    for p in chan_peers:
        pl.semaphore_signal(barrier, inc=1, device_id={"chan": p}, device_id_type=MESH)
    for b in near + inner_peers + outer_peers:
        pl.semaphore_signal(barrier, inc=1, device_id={"band": b}, device_id_type=MESH)

    def to_chan(src_of, dst):
        return [remote(src_of(p), dst, {"chan": p}) for p in chan_peers]

    def swap_rows(src, dst):
        size, lanes = dst.shape[0], src.shape[1]
        copies = to_chan(lambda p: src.at[at(p, size), :], dst.at[:, at(c, lanes)])
        dst[:, at(c, lanes)] = src[at(c, size), :]
        return copies

    def swap_lanes(src, dst):
        size, lanes = src.shape[0], dst.shape[1]
        copies = to_chan(lambda p: src.at[:, at(p, lanes)], dst.at[at(c, size), :])
        dst[at(c, size), :] = src[:, at(c, lanes)]
        return copies

    tail = fin // 16 * 16
    wg_pad[tail:, :] = jnp.zeros((wg_pad.shape[0] - tail, cb), bf16)
    own_w_grid.wait()
    wg_pad[0:fin, :] = w_grid[...]
    wg_t[at(c, cb), :] = flip(wg_pad[...]).astype(bf16)
    pl.semaphore_wait(barrier, len(chan_peers) + len(near) + len(inner_peers) + len(outer_peers))

    core = lax.rem(d, 2)
    sibling = d + 1 - 2 * core

    def wg_half(p):
        return wg_t.at[at(2 * p + core, cb // 2), :]

    wg_copies = to_chan(lambda p: wg_half(c), wg_half(c))

    gpad[tail:, :] = jnp.zeros((gpad.shape[0] - tail, grid_dev), bf16)
    own_grid.wait()
    gpad[0:fin, :] = grid_in[...]
    own_w_gs.wait()
    wgs_t = flip(w_gs[...]).astype(bf16)
    own_mesh.wait()
    for copy in own_rest:
        copy.wait()
    sent(wg_copies)
    mesh_copies = to_chan(lambda p: mesh_in, mesh_full.at[at(c, cb), :])
    gains[c] = jnp.zeros(gains.shape[1:], f32)
    gains[c, 0:1, :] = gain_enc[...]
    gains[c, 1:2, :] = gain_proc[...]
    we_pad[...] = jnp.zeros_like(we_pad)
    we_pad[0:ea, :] = w_ge[...].astype(f32)
    wge_t = jnp.transpose(we_pad[...]).astype(bf16)
    we_pad[0:ea, :] = w_me[...].astype(f32)
    wme_t = jnp.transpose(we_pad[...]).astype(bf16)
    attr_g[...] = jnp.zeros_like(attr_g)
    attr_g[0:ea, :] = g2m_attr[...]
    attr_m[...] = jnp.zeros_like(attr_m)
    attr_m[0:ea, :] = mesh_attr[...]
    wgr_t = flip(w_gr[...]).astype(bf16)
    shared = []
    for k in range(1, nchan):
        arrive([wg_copies[k - 1]])
        piece = wg_half(lax.rem(c - k + nchan, nchan))
        shared.append(remote(piece, piece, {"band": sibling}))
    arrive(shared)

    step = min(256, grid_dev)

    @pl.loop(0, grid_dev // step)
    def _(t):
        cols = at(t, step)
        pre = dot(wg_t[...], gpad[:, cols])
        sig = sigmoid(pre)
        sgrid[:, cols] = sig * (1.0 + pre * (1.0 - sig))
        s_grid[:, cols] = dot(wgs_t, (pre * sig).astype(bf16)).astype(bf16)

    order = [j for o in range(radius, 0, -1) for j in (radius - o, radius + o)]
    passes = [order[i : i + 2] for i in range(0, len(order), 2)]

    def pack(field, send, out, dest):
        rows = field.shape[1]
        copies = []
        for j in order + [radius]:
            picked = dot(field[...], one_hot(send[j : j + 1, :], rows)).astype(bf16)
            if j == radius:
                dest[j * cb : (j + 1) * cb, :] = picked
            else:
                out[j] = picked
                copies.append(remote(out.at[j], dest.at[j * cb : (j + 1) * cb, :], {"band": band_at(j - radius)}))
        return copies

    halo = pack(s_grid, g2m_send, halo_out, table)

    def half_of(shard, full):
        if shard.shape[0] == cb:
            lanes = at(core, width // 2)
            return shard.at[:, lanes], full.at[at(c, cb), lanes], full.at[:, lanes]
        rows = at(core, width // 2)
        return shard.at[rows, :], full.at[rows, at(c, cb)], full.at[rows, :]

    def fetch(pairs):
        pending = []
        for shard, full in pairs:
            src, dst, whole = half_of(shard, full)
            own = fetch_local(src, dst)
            pending.append((own, to_chan(lambda p: src, dst), whole))
        return pending

    def share(pending):
        copies = []
        for own, inbound, whole in pending:
            own.wait()
            arrive(inbound)
            copies.append(remote(whole, whole, {"band": sibling}))
        return copies

    arrive(mesh_copies)
    group_a = fetch([(w_nm, f_nm), (w_na, f_na), (w_no, f_no), (w_ms, f_ms), (w_mr, f_mr)])
    gain_copies = to_chan(lambda p: gains.at[c], gains.at[c])
    cot_copies = to_chan(lambda p: cotangent.at[:, at(p, nb)], cot_rows.at[at(c, cb), :])

    def upper_lower(upper, x):
        return jnp.concatenate([jnp.where(upper, 0.0, x), jnp.where(upper, x, 0.0)], axis=0).astype(bf16)

    def pick_half(upper, pair):
        return jnp.where(upper, pair[cb:], pair[:cb])

    def edges_near(table, recv, w_edge_t, attr, src, dst, grads, tile):
        @pl.loop(0, src.shape[1] // tile)
        def _(t):
            cols = at(t, tile)
            slot, low = slots_of(src[:, cols], table.shape[1], offs)
            upper, node = halves_of(dst[:, cols], half)
            own = dot(table[radius * cb : (radius + 1) * cb, :], one_hot(low, table.shape[1]))
            pre = jnp.where(slot == radius, own, 0.0) + dot(w_edge_t, attr[:, cols])
            grads[:, cols] = pre + pick_half(upper, dot(recv, one_hot(node, half)))

    def edges_far(table, src, dst, grads, tile):
        acc[...] = jnp.zeros_like(acc)

        @pl.loop(0, src.shape[1] // tile)
        def _(t):
            cols = at(t, tile)
            slot, low = slots_of(src[:, cols], table.shape[1], offs)
            upper, node = halves_of(dst[:, cols], half)
            by_src = one_hot(low, table.shape[1])
            below = dot(table[: radius * cb, :], by_src)
            above = dot(table[(radius + 1) * cb :, :], by_src)
            sender = jnp.zeros((cb, tile), f32)
            for j in range(radius):
                sender = jnp.where(slot == j, below[j * cb : (j + 1) * cb, :], sender)
                sender = jnp.where(slot == j + radius + 1, above[j * cb : (j + 1) * cb, :], sender)
            pre = grads[:, cols] + sender
            sig = sigmoid(pre)
            grads[:, cols] = sig * (1.0 + pre * (1.0 - sig))
            acc[...] += dot_nt(one_hot(node, half), upper_lower(upper, pre * sig))

    def nodes_of(out):
        out[:half, :] = acc[:, :cb].astype(bf16)
        out[half:, :] = acc[:, cb:].astype(bf16)

    def edges_backward(grad, src, dst, grads, back, rows_ref, out, inbound, tile):
        capacity, tiles = rows_ref.shape[1], src.shape[1] // tile
        acc[...] = jnp.zeros_like(acc)
        rows_ref[...] = jnp.zeros_like(rows_ref)
        copies = []

        def add_rows(slots, base, cols, d_pre):
            slot, low = slots_of(src[:, cols], capacity, offs)
            slot = slot.astype(jnp.int16)
            parts = [jnp.where(slot == j, d_pre, jnp.zeros((), bf16)) for j in slots]
            rows_ref[base : base + len(slots) * cb, :] += dot_nt(
                jnp.concatenate(parts, axis=0) if len(parts) > 1 else parts[0], one_hot(low, capacity)
            )

        for i, slots in enumerate(passes):
            base = 2 * i * cb

            @pl.loop(0, tiles)
            def _(t):
                cols = at(t, tile)
                if i == 0:
                    upper, node = halves_of(dst[:, cols], half)
                    d_pre = pick_half(upper, dot(grad, one_hot(node, half))) * grads[:, cols]
                    back[:, cols] = d_pre.astype(bf16)
                add_rows(slots, base, cols, back[:, cols])

            for n, j in enumerate(slots):
                out[j] = rows_ref[base + n * cb : base + (n + 1) * cb, :].astype(bf16)
                copies.append(remote(out.at[j], inbound.at[j], {"band": band_at(radius - j)}))

        base = 2 * len(passes) * cb

        @pl.loop(0, tiles)
        def _(t):
            cols = at(t, tile)
            d_pre = back[:, cols]
            upper, node = halves_of(dst[:, cols], half)
            acc[...] += dot_nt(one_hot(node, half), upper_lower(upper, d_pre.astype(f32)))
            add_rows([radius], base, cols, d_pre)

        inbound[radius] = rows_ref[base : base + cb, :].astype(bf16)
        return copies

    tile_g = min(4096, g2m_src.shape[1])
    tile_m = min(4096, mesh_src.shape[1])
    recv_g = two_rows(dot(wgr_t, mesh_full[...]).astype(bf16))
    edges_near(table, recv_g, wge_t, attr_g, g2m_src, g2m_dst, edge_grad, tile_g)
    arrive(halo)
    edges_far(table, g2m_src, g2m_dst, edge_grad, tile_g)
    nodes_of(nbuf)
    enc_copies = swap_rows(nbuf, enc_g)
    a_copies = share(group_a)

    x = flip(mesh_full[:, at(c, nb)])
    arrive(gain_copies)
    gain_e = jnp.concatenate([gains[k, 0:1, :] for k in range(nchan)], axis=1)
    gain_p = jnp.concatenate([gains[k, 1:2, :] for k in range(nchan)], axis=1)
    arrive(a_copies)
    arrive(enc_copies)

    def mlp(latent, gathered, w_l, w_g, w_o):
        pre = dot(latent, w_l[...]) + dot(gathered[...], w_g[...])
        sig = sigmoid(pre)
        out = dot((pre * sig).astype(bf16), w_o[...])
        normed, inverse = norm(out)
        return sig * (1.0 + pre * (1.0 - sig)), normed, inverse

    enc_sg, enc_normed, enc_inverse = mlp(x.astype(bf16), enc_g, f_nm, f_na, f_no)
    mid = (x + enc_normed * gain_e).astype(bf16)
    s_out[...] = dot(mid, f_ms[...]).astype(bf16)
    s_copies = swap_lanes(s_out, s_in)
    r_out[...] = dot(mid, f_mr[...]).astype(bf16)
    r_copies = swap_lanes(r_out, r_in)

    arrive(s_copies)
    mid_s[...] = flip(s_in[...]).astype(bf16)
    m_halo = pack(mid_s, mesh_send, m_halo_out, m_table)
    arrive(r_copies)
    group_b = fetch([(w_pm, f_pm), (w_pa, f_pa), (w_po, f_po)])
    recv_m = two_rows(flip(r_in[...]).astype(bf16))
    edges_near(m_table, recv_m, wme_t, attr_m, mesh_src, mesh_dst, m_edge_grad, tile_m)
    arrive(m_halo)
    edges_far(m_table, mesh_src, mesh_dst, m_edge_grad, tile_m)
    nodes_of(m_nbuf)
    proc_copies = swap_rows(m_nbuf, proc_g)
    b_copies = share(group_b)
    arrive(cot_copies)
    cot = flip(cot_rows[...])
    arrive(b_copies)
    arrive(proc_copies)

    proc_sg, proc_normed, proc_inverse = mlp(mid, proc_g, f_pm, f_pa, f_po)
    d_out = norm_back(cot, proc_normed, proc_inverse, gain_p)
    d_hid = (dot_nt(d_out, f_po[...]) * proc_sg).astype(bf16)
    dg_out[...] = dot_nt(d_hid, f_pa[...]).astype(bf16)
    dg_copies = swap_lanes(dg_out, dg_in)
    mo_out[...] = flip(mid.astype(f32) + proc_normed * gain_p).astype(bf16)
    d_mid = cot + dot_nt(d_hid, f_pm[...])
    arrive(dg_copies)
    group_c = fetch([(w_gr, f_gr), (w_gs, f_gs)])
    mo_copies = swap_rows(mo_out, mo_in)
    m_back = edges_backward(
        two_rows(flip(dg_in[...]).astype(bf16)), mesh_src, mesh_dst, m_edge_grad, m_edge_back,
        rows_acc, m_back_out, m_back_in, tile_m,
    )
    nodes_of(mr_out)
    mr_copies = swap_rows(mr_out, mr_in)

    def gather_back(copies, inbound, add):
        value = add(radius, inbound[radius])
        for j, copy in zip(order, copies):
            arrive([copy])
            value = value + add(j, inbound[j])
        return value

    h_out[...] = gather_back(
        m_back, m_back_in, lambda j, rows: dot_nt(one_hot(mesh_send[j : j + 1, :], mesh_dev), rows)
    ).astype(bf16)
    h_copies = swap_rows(h_out, h_in)
    c_copies = share(group_c)
    arrive(mr_copies)
    d_mid = d_mid + dot_nt(mr_in[...], f_mr[...])
    arrive(h_copies)
    d_mid = d_mid + dot_nt(h_in[...], f_ms[...])

    d_out = norm_back(d_mid, enc_normed, enc_inverse, gain_e)
    d_hid = (dot_nt(d_out, f_no[...]) * enc_sg).astype(bf16)
    de_out[...] = dot_nt(d_hid, f_na[...]).astype(bf16)
    de_copies = swap_lanes(de_out, de_in)
    d_mesh = d_mid + dot_nt(d_hid, f_nm[...])
    arrive(de_copies)

    g_back = edges_backward(
        two_rows(flip(de_in[...]).astype(bf16)), g2m_src, g2m_dst, edge_grad, edge_back,
        g_rows_acc, g_back_out, g_back_in, tile_g,
    )
    nodes_of(er_out)
    er_copies = swap_rows(er_out, er_in)
    arrive(c_copies)
    dgrid_out[...] = gather_back(
        g_back, g_back_in, lambda j, rows: dot_nt(rows, one_hot(g2m_send[j : j + 1, :], grid_dev))
    ).astype(bf16)
    dgrid_copies = swap_lanes(dgrid_out, dgrid_in)
    arrive(er_copies)
    mg_out[...] = jnp.transpose(d_mesh + dot_nt(er_in[...], f_gr[...]))
    arrive(dgrid_copies)
    dpre_out[...] = (dot(f_gs[...], dgrid_in[...]) * sgrid[:, at(c, gb)]).astype(bf16)
    dpre_copies = swap_rows(dpre_out, dpre_in)
    arrive(mo_copies)
    mesh_out[...] = mo_in[...]
    arrive(dpre_copies)

    part[...] = dot_nt(gpad[...], dpre_in[...]).astype(bf16)
    piece = part.shape[0] // inner
    first = []
    for k in range(1, inner):
        q = lax.rem(place + k, inner)
        first.append(remote(part.at[at(q, piece), :], rs1.at[place], {"band": inner_peers[k - 1]}))
    mg_copies = swap_rows(mg_out, mg_in)
    rs1[place] = part[at(place, piece), :]
    arrive(first)
    mine[...] = jnp.sum(rs1[...].astype(f32), axis=0)
    rs2[group] = mine[...]
    second = [remote(mine, rs2.at[group], {"band": b}) for b in outer_peers]
    arrive(mg_copies)
    mesh_grad[...] = mg_in[...]
    arrive(second)
    last[...] = (jnp.sum(rs2[...], axis=0) * scale).astype(bf16)
    total[at(place, piece), :] = last[...]
    third = [remote(last, total.at[at(place, piece), :], {"band": b}) for b in inner_peers]
    arrive(third)
    w_grid_grad[...] = total[0:fin, :].astype(f32)
    for copy in started:
        copy.wait_send()


def local(nband, nchan, inner, *args):
    names = INPUTS
    a = dict(zip(names, args))
    for name in ("g2m_src", "g2m_dst", "mesh_src", "mesh_dst", "gain_enc", "gain_proc"):
        a[name] = a[name].reshape(1, -1)
    fin, grid_dev = a["grid_in"].shape
    width, cb = a["w_gs"].shape
    mesh_dev = a["mesh_in"].shape[1]
    nb, gb = mesh_dev // nchan, grid_dev // nchan
    offs, cap = a["g2m_send"].shape
    mcap = a["mesh_send"].shape[1]
    edges, medges = a["g2m_src"].shape[1], a["mesh_src"].shape[1]
    fp = -(-fin // 128) * 128
    scale = float(grid_dev * nband) ** (-0.5)
    v = pltpu.VMEM
    full = v((width, width), bf16)
    nodes = v((mesh_dev, cb), bf16)
    block = v((nb, width), bf16)
    held = [
        *("grid_in", "w_grid", "g2m_attr", "g2m_send", "g2m_src", "g2m_dst", "w_gs", "w_gr", "w_ge", "gain_enc"),
        *("mesh_attr", "mesh_send", "mesh_src", "mesh_dst", "w_me", "gain_proc"),
    ]
    scratch = [
        *[v(a[name].shape, a[name].dtype) for name in held],
        v((fp, grid_dev), bf16), v((fp, cb), bf16), v((width, fp), bf16), v((16, cb), f32),
        v((16, edges), bf16), v((16, medges), bf16),
        v((width, mesh_dev), bf16), v((nchan, 8, cb), f32), v((width, nb), bf16),
        *[full] * 10,
        v((width, grid_dev), f32), v((cb, grid_dev), bf16), v((offs, cb, cap), bf16), v((offs * cb, cap), bf16),
        v((cb, edges), f32), v((cb, edges), bf16),
        v((mesh_dev // 2, 2 * cb), f32), nodes, block,
        block, block, nodes, nodes, v((cb, mesh_dev), bf16), v((offs, cb, mcap), bf16), v((offs * cb, mcap), bf16),
        v((cb, medges), f32), v((cb, medges), bf16), nodes, block,
        v((width, nb), bf16), v((cb, mesh_dev), bf16), block, nodes, v((offs * cb, mcap), f32),
        v((offs, cb, mcap), bf16), v((offs, cb, mcap), bf16), nodes, block, nodes, block,
        block, nodes, v((offs * cb, cap), f32), v((offs, cb, cap), bf16), v((offs, cb, cap), bf16), nodes, block,
        v((width, nb), f32), v((cb, mesh_dev), f32),
        v((cb, grid_dev), bf16), v((width, gb), bf16), v((width, gb), bf16), v((cb, grid_dev), bf16),
        v((fp, cb), bf16), v((inner, fp // inner, cb), bf16), v((fp // inner, cb), f32),
        v((nband // inner, fp // inner, cb), f32), v((fp // inner, cb), bf16), v((fp, cb), bf16),
        pltpu.SemaphoreType.DMA((SEMS,)), pltpu.SemaphoreType.DMA((SEMS,)), pltpu.SemaphoreType.DMA((32,)),
    ]
    spec = pl.BlockSpec(memory_space=pltpu.VMEM)
    return pl.pallas_call(
        functools.partial(kernel, nband, nchan, inner, scale),
        out_shape=(
            jax.ShapeDtypeStruct((cb, mesh_dev), bf16),
            jax.ShapeDtypeStruct((cb, mesh_dev), f32),
            jax.ShapeDtypeStruct((fin, cb), f32),
        ),
        in_specs=[pl.BlockSpec(memory_space=pl.ANY)] * len(names),
        out_specs=(spec,) * 3,
        scratch_shapes=scratch,
        compiler_params=pltpu.CompilerParams(
            collective_id=0, has_side_effects=True, vmem_limit_bytes=56 * 2**20
        ),
    )(*[a[name] for name in names])


def solution(mesh):
    nband, nchan = mesh.shape["band"], mesh.shape["chan"]
    inner = min(16, nband // 2)
    return jax.shard_map(
        functools.partial(local, nband, nchan, inner),
        mesh=mesh,
        in_specs=(
            P(None, "band"),
            P(None, "chan"),
            P("chan", "band"),
            P(None, "band"),
            P("band", None),
            P("band"),
            P("band"),
            P(None, "chan"),
            P(None, "chan"),
            P(None, "chan"),
            P("chan", None),
            P("chan", None),
            P("chan", None),
            P("chan"),
            P(None, "band"),
            P("band", None),
            P("band"),
            P("band"),
            P(None, "chan"),
            P(None, "chan"),
            P(None, "chan"),
            P("chan", None),
            P("chan", None),
            P("chan", None),
            P("chan"),
            P("chan", "band"),
        ),
        out_specs=(P("chan", "band"), P("chan", "band"), P(None, "chan")),
        check_vma=False,
    )
```

time: 1070 us -> 131 us (0.12)
  waiting for transfers between devices: 327 us -> 0 us
  other arithmetic: 309 us -> 0 us
  local copies, waits for them, and re-layouts: 211 us -> 3.34 us
  Pallas kernels: 0 us -> 127 us
  blocking collectives: 90.7 us -> 0 us
  starting transfers between devices: 74.2 us -> 0 us
  matrix products: 33.1 us -> 0 us
  between operations: 15.4 us -> 0.66 us
    scatter-add x16 -> x0, other arithmetic: 268 us -> none  [the longest x6 229 us: column_sum(): return totals.at[:, safe_ids].add(values.astype(jnp.float32), mode='drop')]
    psum x1 -> x0, waiting for transfers between devices: 178 us -> none  [local(): w_grid_grad = lax.psum(w_part, 'band') * grad_scale]
    gather x22 -> x0, local copies, waits for them, and re-layouts: 170 us -> none  [the longest x4 50.6 us: edge_sums(): jnp.take(d_gather, anchors, axis=1)]
    reduce_scatter x7 -> x0, waiting for transfers between devices: 141 us -> none  [the longest x4 93.9 us: split_channels(): lax.psum_scatter(term_fn(jnp.int32(0), chan_share * lax.axis_size('chan')...]
    pallas_call x0 -> x1, Pallas kernels: none -> 127 us  [local(): pl.pallas_call(functools.partial(kernel, nband, nchan, inner, scale), out...]
    ppermute x16 -> x0, starting transfers between devices: 73.9 us -> none  [from_behind(): return lax.ppermute(block, axis, route)]
    all_gather x6 -> x0, blocking collectives: 63.3 us -> none  [the longest x2 20.6 us: split_channels(): d_pre_full = lax.all_gather(d_pre, 'chan', axis=0, tiled=True)]
    dot_general x24 -> x0, matrix products: 33.1 us -> none  [the longest x13 19.8 us: contract(): lax.dot_general(weight, field_in, (((0,), (0,)), ((), ())), preferred_ele...]
  transfers between devices with their start and end apart: 25 -> 0, of which waited for: 10 -> 0; matrix products, arithmetic and copies ran while one was open for 18% -> 0% of each run, Pallas kernels for 0% -> 0%
where the time goes in v1:
time: 131 us
  Pallas kernels  127 us (97%)
  local copies, waits for them, and re-layouts  3.34 us (3%)
    pallas_call x1, Pallas kernels, local(): pl.pallas_call(functools.partial(kernel, nband, nchan, inner, scale), out...  127 us
    unnamed x7, local copies, waits for them, and re-layouts  3.34 us

profile of v1, /device:TPU:1, one launch (start us, length us, event | category | flops | bytes accessed | tf_op | source)
XLA Modules:
  0.0 130.7 jit_solution(16688175074198927425)
XLA Ops:
  0.6 126.7 %shard_map.265 = (bf16[128,512]{1,0:T(8,128)(2,1)}, f32[128,512]{1,0:T(8,128)}, f32[474,128]{1,0:T(8,128)}) custom-call(bf16[474,1024]{1,0:T(8,128)(2,1)} %grid_hbm.1, bf16[474,128]{1,0:T(8,128)(2,1)} %w_grid_hbm.1, bf16[128,512]{1,0:T(8,128)(2,1)} %mesh_in.1, bf16[4,8192]{1,0:T(4,128)(2,1)} %g2m_attr_hbm.1, s32[5,512]{1,0:T(8,128)} %g2m_send_hbm.1, ...), custom_call_target="tpu_custom_call" | custom-call | tf_op jit(solution)/shard_map/pallas_call | solution.py:545
  127.4 0.0 copy-start
  127.4 1.6 %copy.32 = bf16[128,512]{1,0:T(8,128)(2,1)} copy(bf16[128,512]{1,0:T(8,128)(2,1)} %get-tuple-element.6) | data formatting | bytes 262144
  129.0 0.0 copy-done
  129.0 0.0 copy-start.1
  129.0 0.7 copy.33
  129.7 0.3 copy-done.1
  130.0 0.7 copy.34
Async XLA Ops:
  127.4 1.6 %copy-start = (f32[128,512]{1,0:T(8,128)S(1)}, f32[128,512]{1,0:T(8,128)}, u32[]{:S(2)}) copy-start(f32[128,512]{1,0:T(8,128)} %get-tuple-element.7) | copy-start | bytes 786436
  129.0 1.0 copy-start.1

commit v2 on v1

--- a/solution.py
+++ b/solution.py
@@ -11,7 +11,7 @@
 bf16 = jnp.bfloat16
 f32 = jnp.float32
 MESH = pl.DeviceIdType.MESH
-SEMS = 192
+BATCHES, OWN = 40, 22
 INPUTS = (
     *("grid_in", "w_grid", "mesh_in", "g2m_attr", "g2m_send", "g2m_src", "g2m_dst"),
     *("w_gs", "w_gr", "w_ge", "w_nm", "w_na", "w_no", "gain_enc"),
@@ -20,6 +20,10 @@
 )
 
 
+def whole(f):
+    return f[...].reshape(f.shape[0] * f.shape[1], f.shape[2])
+
+
 def dot(a, b):
     return jnp.dot(a, b, preferred_element_type=f32)
 
@@ -80,22 +84,24 @@
     w_gs_hbm, w_gr_hbm, w_ge_hbm, w_nm, w_na, w_no, gain_enc_hbm,
     mesh_attr_hbm, mesh_send_hbm, mesh_src_hbm, mesh_dst_hbm,
     w_ms, w_mr, w_me_hbm, w_pm, w_pa, w_po, gain_proc_hbm, cotangent,
-    mesh_out, mesh_grad, w_grid_grad,
+    mesh_out, mesh_grad, w_grid_sum,
     grid_in, w_grid, g2m_attr, g2m_send, g2m_src, g2m_dst, w_gs, w_gr, w_ge, gain_enc,
     mesh_attr, mesh_send, mesh_src, mesh_dst, w_me, gain_proc,
     gpad, wg_pad, wg_t, we_pad, attr_g, attr_m,
     mesh_full, gains, cot_rows,
-    f_nm, f_na, f_no, f_pm, f_pa, f_po, f_gs, f_gr, f_ms, f_mr,
+    f_all,
     sgrid, s_grid, halo_out, table, edge_grad, edge_back,
     acc, nbuf, enc_g,
     s_out, r_out, s_in, r_in, mid_s, m_halo_out, m_table, m_edge_grad, m_edge_back, m_nbuf, proc_g,
     mo_out, mo_in, dg_out, dg_in, rows_acc, m_back_out, m_back_in, mr_out, mr_in, h_out, h_in,
     de_out, de_in, g_rows_acc, g_back_out, g_back_in, er_out, er_in, mg_out, mg_in,
     dgrid_out, dgrid_in, dpre_out, dpre_in,
-    part, rs1, mine, rs2, last, total,
+    part, pair_in, pair_sum, rs1, mine, rs2, total,
     ssem, rsem, lsem,
 ):
     d, c = lax.axis_index("band"), lax.axis_index("chan")
+    core = lax.rem(d, 2)
+    sibling = d + 1 - 2 * core
     width, cb = w_gs.shape
     fin, grid_dev = grid_in.shape
     mesh_dev = mesh_in.shape[1]
@@ -105,6 +111,9 @@
     offs, cap = g2m_send.shape
     radius = offs // 2
     ea = w_ge.shape[0]
+    f_nm, f_na, f_no, f_ms, f_mr, f_pm, f_pa, f_po, f_gs, f_gr = (
+        f_all.at[i] for i in range(10)
+    )
     count = [0]
     local_count = [0]
     started = []
@@ -118,25 +127,30 @@
         copy.start()
         return copy
 
-    def remote(src, dst, target):
+    def wait_on(whole, i):
+        return pltpu.make_async_remote_copy(
+            src_ref=whole, dst_ref=whole, send_sem=ssem.at[i], recv_sem=rsem.at[i],
+            device_id={"band": sibling}, device_id_type=MESH,
+        )
+
+    def send(sends, whole):
         i = count[0]
         count[0] += 1
-        copy = pltpu.make_async_remote_copy(
-            src_ref=src, dst_ref=dst, send_sem=ssem.at[i], recv_sem=rsem.at[i],
-            device_id=target, device_id_type=MESH,
-        )
-        copy.start()
-        started.append(copy)
-        return copy
-
-    def sent(copies):
-        for copy in copies:
-            copy.wait_send()
-            started[:] = [other for other in started if other is not copy]
-
-    def arrive(copies):
-        for copy in copies:
-            copy.wait_recv()
+        for src, dst, target in sends:
+            pltpu.make_async_remote_copy(
+                src_ref=src, dst_ref=dst, send_sem=ssem.at[i], recv_sem=rsem.at[i],
+                device_id=target, device_id_type=MESH,
+            ).start()
+        batch = (whole, i)
+        started.append(batch)
+        return batch
+
+    def sent(batch):
+        wait_on(*batch).wait_send()
+        started[:] = [other for other in started if other is not batch]
+
+    def arrive(batch):
+        wait_on(*batch).wait_recv()
 
     own_w_grid = fetch_local(w_grid_hbm, w_grid)
     own_w_gs = fetch_local(w_gs_hbm, w_gs)
@@ -152,51 +166,57 @@
         )
     ]
 
-    chan_peers = [lax.rem(c + k, nchan) for k in range(1, nchan)]
+    def far_first(size):
+        return sorted(range(1, size), key=lambda k: -min(k, size - k))
+
+    chan_peers = [lax.rem(c + k, nchan) for k in far_first(nchan)]
 
     def band_at(offset):
         return lax.rem(d + offset + nband, nband)
 
     near = [band_at(o) for o in range(-radius, radius + 1) if o != 0]
     group, place = d // inner, lax.rem(d, inner)
-    inner_peers = [group * inner + lax.rem(place + k, inner) for k in range(1, inner)]
+    row, rows = place // 2, inner // 2
+    row_peers = [lax.rem(row + k, rows) for k in far_first(rows)]
+    inner_peers = [group * inner + 2 * p + core for p in row_peers]
     outer = nband // inner
-    outer_peers = [lax.rem(group + k, outer) * inner + place for k in range(1, outer)]
+    outer_peers = [lax.rem(group + k, outer) * inner + place for k in far_first(outer)]
+    met = near + inner_peers + outer_peers + [sibling]
     barrier = pltpu.get_barrier_semaphore()
     for p in chan_peers:
         pl.semaphore_signal(barrier, inc=1, device_id={"chan": p}, device_id_type=MESH)
-    for b in near + inner_peers + outer_peers:
+    for b in met:
         pl.semaphore_signal(barrier, inc=1, device_id={"band": b}, device_id_type=MESH)
 
-    def to_chan(src_of, dst):
-        return [remote(src_of(p), dst, {"chan": p}) for p in chan_peers]
+    others = nchan - 1
+
+    def to_chan(src_of, dst, whole):
+        return send([(src_of(p), dst, {"chan": p}) for p in chan_peers], whole)
 
     def swap_rows(src, dst):
         size, lanes = dst.shape[0], src.shape[1]
-        copies = to_chan(lambda p: src.at[at(p, size), :], dst.at[:, at(c, lanes)])
+        batch = to_chan(lambda p: src.at[at(p, size), :], dst.at[:, at(c, lanes)], dst.at[:, : others * lanes])
         dst[:, at(c, lanes)] = src[at(c, size), :]
-        return copies
+        return batch
 
     def swap_lanes(src, dst):
         size, lanes = src.shape[0], dst.shape[1]
-        copies = to_chan(lambda p: src.at[:, at(p, lanes)], dst.at[at(c, size), :])
+        batch = to_chan(lambda p: src.at[:, at(p, lanes)], dst.at[at(c, size), :], dst.at[: others * size, :])
         dst[at(c, size), :] = src[:, at(c, lanes)]
-        return copies
+        return batch
 
     tail = fin // 16 * 16
     wg_pad[tail:, :] = jnp.zeros((wg_pad.shape[0] - tail, cb), bf16)
     own_w_grid.wait()
     wg_pad[0:fin, :] = w_grid[...]
     wg_t[at(c, cb), :] = flip(wg_pad[...]).astype(bf16)
-    pl.semaphore_wait(barrier, len(chan_peers) + len(near) + len(inner_peers) + len(outer_peers))
-
-    core = lax.rem(d, 2)
-    sibling = d + 1 - 2 * core
+    pl.semaphore_wait(barrier, len(chan_peers) + len(met))
 
     def wg_half(p):
         return wg_t.at[at(2 * p + core, cb // 2), :]
 
-    wg_copies = to_chan(lambda p: wg_half(c), wg_half(c))
+    wg_copies = to_chan(lambda p: wg_half(c), wg_half(c), wg_t.at[: others * cb // 2, :])
+    gains[c] = jnp.zeros(gains.shape[1:], f32)
 
     gpad[tail:, :] = jnp.zeros((gpad.shape[0] - tail, grid_dev), bf16)
     own_grid.wait()
@@ -207,8 +227,7 @@
     for copy in own_rest:
         copy.wait()
     sent(wg_copies)
-    mesh_copies = to_chan(lambda p: mesh_in, mesh_full.at[at(c, cb), :])
-    gains[c] = jnp.zeros(gains.shape[1:], f32)
+    mesh_copies = to_chan(lambda p: mesh_in, mesh_full.at[at(c, cb), :], mesh_full.at[: others * cb, :])
     gains[c, 0:1, :] = gain_enc[...]
     gains[c, 1:2, :] = gain_proc[...]
     we_pad[...] = jnp.zeros_like(we_pad)
@@ -221,12 +240,9 @@
     attr_m[...] = jnp.zeros_like(attr_m)
     attr_m[0:ea, :] = mesh_attr[...]
     wgr_t = flip(w_gr[...]).astype(bf16)
-    shared = []
-    for k in range(1, nchan):
-        arrive([wg_copies[k - 1]])
-        piece = wg_half(lax.rem(c - k + nchan, nchan))
-        shared.append(remote(piece, piece, {"band": sibling}))
-    arrive(shared)
+    arrive(wg_copies)
+    halves = [wg_half(p) for p in chan_peers]
+    arrive(send([(half_block, half_block, {"band": sibling}) for half_block in halves], wg_t.at[: others * cb // 2, :]))
 
     step = min(256, grid_dev)
 
@@ -241,47 +257,86 @@
     order = [j for o in range(radius, 0, -1) for j in (radius - o, radius + o)]
     passes = [order[i : i + 2] for i in range(0, len(order), 2)]
 
-    def pack(field, send, out, dest):
-        rows = field.shape[1]
-        copies = []
-        for j in order + [radius]:
-            picked = dot(field[...], one_hot(send[j : j + 1, :], rows)).astype(bf16)
-            if j == radius:
-                dest[j * cb : (j + 1) * cb, :] = picked
-            else:
-                out[j] = picked
-                copies.append(remote(out.at[j], dest.at[j * cb : (j + 1) * cb, :], {"band": band_at(j - radius)}))
-        return copies
+    def pack(field, lists, out, dest):
+        def picked(j):
+            return dot(field[...], one_hot(lists[j : j + 1, :], field.shape[1])).astype(bf16)
+
+        def block(j):
+            return dest.at[j * cb : (j + 1) * cb, :]
+
+        def sends():
+            for j in order:
+                out[j] = picked(j)
+                yield out.at[j], block(j), {"band": band_at(j - radius)}
+
+        batch = send(sends(), dest.at[: (offs - 1) * cb, :])
+        dest[radius * cb : (radius + 1) * cb, :] = picked(radius)
+        return batch
 
     halo = pack(s_grid, g2m_send, halo_out, table)
 
-    def half_of(shard, full):
+    def part_of(shard, full, cuts):
+        index = group if cuts > 1 else 0
         if shard.shape[0] == cb:
-            lanes = at(core, width // 2)
-            return shard.at[:, lanes], full.at[at(c, cb), lanes], full.at[:, lanes]
-        rows = at(core, width // 2)
-        return shard.at[rows, :], full.at[rows, at(c, cb)], full.at[rows, :]
-
-    def fetch(pairs):
-        pending = []
+            rows, lanes = at(index, cb // cuts), at(core, width // 2)
+            return shard.at[rows, lanes], full.at[c, rows, lanes], full.at[:, rows, lanes], full.at[:, :, lanes]
+        blocks = at(core, nchan // 2)
+        size = width // 2 // cuts
+        if size >= cb:
+            blocks, rows = at(core * cuts + index, size // cb), pl.ds(0, cb)
+        else:
+            first = (core * cuts + index) * size
+            blocks, rows = pl.ds(first // cb, 1), pl.ds(pl.multiple_of(lax.rem(first, cb), size), size)
+        source = shard.at[at(core * cuts + index, size), :]
+        if size >= cb:
+            source = [shard.at[at((core * cuts + index) * (size // cb) + n, cb), :] for n in range(size // cb)]
+            target = [full.at[(core * cuts + index) * (size // cb) + n, :, at(c, cb)] for n in range(size // cb)]
+        else:
+            source, target = [source], [full.at[first // cb, rows, at(c, cb)]]
+        return source, target, full.at[blocks, rows, :], full.at[at(core, nchan // 2), :, :]
+
+    def listed(x):
+        return x if isinstance(x, list) else [x]
+
+    def fetch(pairs, cuts=1):
+        sends, regions, halves, own = [], [], [], local_count[0]
+        local_count[0] += 1
         for shard, full in pairs:
-            src, dst, whole = half_of(shard, full)
-            own = fetch_local(src, dst)
-            pending.append((own, to_chan(lambda p: src, dst), whole))
-        return pending
-
-    def share(pending):
-        copies = []
-        for own, inbound, whole in pending:
-            own.wait()
-            arrive(inbound)
-            copies.append(remote(whole, whole, {"band": sibling}))
-        return copies
-
-    arrive(mesh_copies)
-    group_a = fetch([(w_nm, f_nm), (w_na, f_na), (w_no, f_no), (w_ms, f_ms), (w_mr, f_mr)])
-    gain_copies = to_chan(lambda p: gains.at[c], gains.at[c])
-    cot_copies = to_chan(lambda p: cotangent.at[:, at(p, nb)], cot_rows.at[at(c, cb), :])
+            src, dst, region, whole = part_of(shard, full, cuts)
+            for one, other in zip(listed(src), listed(dst)):
+                pltpu.make_async_copy(one, other, lsem.at[own]).start()
+                sends += [(one, other, {"chan": p}) for p in chan_peers]
+            regions.append(region)
+            halves.append(whole)
+        unit = cb // 2 // cuts
+        size = len(pairs)
+        return send(sends, f_all.at[:size, :others, :unit, :]), own, f_all.at[:size, 0, :unit, :], regions, halves
+
+    def fetched(group_copies):
+        inbound, own, own_whole, regions, halves = group_copies
+        pltpu.make_async_copy(own_whole, own_whole, lsem.at[own]).wait()
+        arrive(inbound)
+        return regions, halves
+
+    def relay(group_copies):
+        regions, halves = fetched(group_copies)
+        sends = [(r, r, {"band": b}) for r in regions for b in outer_peers]
+        unit = nchan * cb // 2 // outer
+        return send(sends, f_all.at[: len(regions), : outer - 1, :unit, :]), halves
+
+    def share(halves):
+        return send([(w, w, {"band": sibling}) for w in halves], f_all.at[: len(halves), : nchan // 2, :, :])
+
+    def relayed(relay_copies):
+        arrive(relay_copies[0])
+        return share(relay_copies[1])
+
+    sent(mesh_copies)
+    gain_copies = to_chan(lambda p: gains.at[c], gains.at[c], gains.at[:others])
+    group_m = fetch([(w_ms, f_ms), (w_mr, f_mr)], outer)
+    group_a = fetch([(w_nm, f_nm), (w_na, f_na), (w_no, f_no)])
+    group_b = fetch([(w_pm, f_pm), (w_pa, f_pa), (w_po, f_po)], outer)
+    group_c = fetch([(w_gr, f_gr), (w_gs, f_gs)], outer)
 
     def upper_lower(upper, x):
         return jnp.concatenate([jnp.where(upper, 0.0, x), jnp.where(upper, x, 0.0)], axis=0).astype(bf16)
@@ -351,7 +406,8 @@
 
             for n, j in enumerate(slots):
                 out[j] = rows_ref[base + n * cb : base + (n + 1) * cb, :].astype(bf16)
-                copies.append(remote(out.at[j], inbound.at[j], {"band": band_at(radius - j)}))
+            sends = [(out.at[j], inbound.at[j], {"band": band_at(radius - j)}) for j in slots]
+            copies.append(send(sends, inbound.at[: len(slots)]))
 
         base = 2 * len(passes) * cb
 
@@ -368,64 +424,73 @@
 
     tile_g = min(4096, g2m_src.shape[1])
     tile_m = min(4096, mesh_src.shape[1])
+    arrive(mesh_copies)
     recv_g = two_rows(dot(wgr_t, mesh_full[...]).astype(bf16))
     edges_near(table, recv_g, wge_t, attr_g, g2m_src, g2m_dst, edge_grad, tile_g)
+    m_relay = relay(group_m)
     arrive(halo)
     edges_far(table, g2m_src, g2m_dst, edge_grad, tile_g)
     nodes_of(nbuf)
     enc_copies = swap_rows(nbuf, enc_g)
-    a_copies = share(group_a)
+    a_copies = share(fetched(group_a)[1])
+    b_relay = relay(group_b)
+    m_copies = relayed(m_relay)
 
     x = flip(mesh_full[:, at(c, nb)])
     arrive(gain_copies)
     gain_e = jnp.concatenate([gains[k, 0:1, :] for k in range(nchan)], axis=1)
     gain_p = jnp.concatenate([gains[k, 1:2, :] for k in range(nchan)], axis=1)
     arrive(a_copies)
-    arrive(enc_copies)
-
-    def mlp(latent, gathered, w_l, w_g, w_o):
-        pre = dot(latent, w_l[...]) + dot(gathered[...], w_g[...])
+
+    def mlp(pre, w_o):
         sig = sigmoid(pre)
-        out = dot((pre * sig).astype(bf16), w_o[...])
+        out = dot((pre * sig).astype(bf16), whole(w_o))
         normed, inverse = norm(out)
         return sig * (1.0 + pre * (1.0 - sig)), normed, inverse
 
-    enc_sg, enc_normed, enc_inverse = mlp(x.astype(bf16), enc_g, f_nm, f_na, f_no)
+    pre = dot(x.astype(bf16), whole(f_nm))
+    arrive(enc_copies)
+    enc_sg, enc_normed, enc_inverse = mlp(pre + dot(enc_g[...], whole(f_na)), f_no)
     mid = (x + enc_normed * gain_e).astype(bf16)
-    s_out[...] = dot(mid, f_ms[...]).astype(bf16)
+    arrive(m_copies)
+    s_out[...] = dot(mid, whole(f_ms)).astype(bf16)
     s_copies = swap_lanes(s_out, s_in)
-    r_out[...] = dot(mid, f_mr[...]).astype(bf16)
+    r_out[...] = dot(mid, whole(f_mr)).astype(bf16)
     r_copies = swap_lanes(r_out, r_in)
 
     arrive(s_copies)
     mid_s[...] = flip(s_in[...]).astype(bf16)
     m_halo = pack(mid_s, mesh_send, m_halo_out, m_table)
     arrive(r_copies)
-    group_b = fetch([(w_pm, f_pm), (w_pa, f_pa), (w_po, f_po)])
+    c_relay = relay(group_c)
+    cot_copies = to_chan(
+        lambda p: cotangent.at[:, at(p, nb)], cot_rows.at[at(c, cb), :], cot_rows.at[: others * cb, :]
+    )
     recv_m = two_rows(flip(r_in[...]).astype(bf16))
     edges_near(m_table, recv_m, wme_t, attr_m, mesh_src, mesh_dst, m_edge_grad, tile_m)
     arrive(m_halo)
     edges_far(m_table, mesh_src, mesh_dst, m_edge_grad, tile_m)
     nodes_of(m_nbuf)
     proc_copies = swap_rows(m_nbuf, proc_g)
-    b_copies = share(group_b)
+    b_copies = relayed(b_relay)
     arrive(cot_copies)
     cot = flip(cot_rows[...])
     arrive(b_copies)
+    pre = dot(mid, whole(f_pm))
     arrive(proc_copies)
 
-    proc_sg, proc_normed, proc_inverse = mlp(mid, proc_g, f_pm, f_pa, f_po)
+    proc_sg, proc_normed, proc_inverse = mlp(pre + dot(proc_g[...], whole(f_pa)), f_po)
     d_out = norm_back(cot, proc_normed, proc_inverse, gain_p)
-    d_hid = (dot_nt(d_out, f_po[...]) * proc_sg).astype(bf16)
-    dg_out[...] = dot_nt(d_hid, f_pa[...]).astype(bf16)
-    dg_copies = swap_lanes(dg_out, dg_in)
+    d_hid = (dot_nt(d_out, whole(f_po)) * proc_sg).astype(bf16)
+    dg_out[...] = dot_nt(whole(f_pa), d_hid).astype(bf16)
+    dg_copies = swap_rows(dg_out, dg_in)
+    c_copies = relayed(c_relay)
     mo_out[...] = flip(mid.astype(f32) + proc_normed * gain_p).astype(bf16)
-    d_mid = cot + dot_nt(d_hid, f_pm[...])
+    d_mid = cot + dot_nt(d_hid, whole(f_pm))
     arrive(dg_copies)
-    group_c = fetch([(w_gr, f_gr), (w_gs, f_gs)])
     mo_copies = swap_rows(mo_out, mo_in)
     m_back = edges_backward(
-        two_rows(flip(dg_in[...]).astype(bf16)), mesh_src, mesh_dst, m_edge_grad, m_edge_back,
+        two_rows(dg_in[...]), mesh_src, mesh_dst, m_edge_grad, m_edge_back,
         rows_acc, m_back_out, m_back_in, tile_m,
     )
     nodes_of(mr_out)
@@ -433,30 +498,30 @@
 
     def gather_back(copies, inbound, add):
         value = add(radius, inbound[radius])
-        for j, copy in zip(order, copies):
-            arrive([copy])
-            value = value + add(j, inbound[j])
+        for slots, batch in zip(passes, copies):
+            arrive(batch)
+            for j in slots:
+                value = value + add(j, inbound[j])
         return value
 
     h_out[...] = gather_back(
         m_back, m_back_in, lambda j, rows: dot_nt(one_hot(mesh_send[j : j + 1, :], mesh_dev), rows)
     ).astype(bf16)
     h_copies = swap_rows(h_out, h_in)
-    c_copies = share(group_c)
     arrive(mr_copies)
-    d_mid = d_mid + dot_nt(mr_in[...], f_mr[...])
+    d_mid = d_mid + dot_nt(mr_in[...], whole(f_mr))
     arrive(h_copies)
-    d_mid = d_mid + dot_nt(h_in[...], f_ms[...])
+    d_mid = d_mid + dot_nt(h_in[...], whole(f_ms))
 
     d_out = norm_back(d_mid, enc_normed, enc_inverse, gain_e)
-    d_hid = (dot_nt(d_out, f_no[...]) * enc_sg).astype(bf16)
-    de_out[...] = dot_nt(d_hid, f_na[...]).astype(bf16)
-    de_copies = swap_lanes(de_out, de_in)
-    d_mesh = d_mid + dot_nt(d_hid, f_nm[...])
+    d_hid = (dot_nt(d_out, whole(f_no)) * enc_sg).astype(bf16)
+    de_out[...] = dot_nt(whole(f_na), d_hid).astype(bf16)
+    de_copies = swap_rows(de_out, de_in)
+    d_mesh = d_mid + dot_nt(d_hid, whole(f_nm))
     arrive(de_copies)
 
     g_back = edges_backward(
-        two_rows(flip(de_in[...]).astype(bf16)), g2m_src, g2m_dst, edge_grad, edge_back,
+        two_rows(de_in[...]), g2m_src, g2m_dst, edge_grad, edge_back,
         g_rows_acc, g_back_out, g_back_in, tile_g,
     )
     nodes_of(er_out)
@@ -467,36 +532,48 @@
     ).astype(bf16)
     dgrid_copies = swap_lanes(dgrid_out, dgrid_in)
     arrive(er_copies)
-    mg_out[...] = jnp.transpose(d_mesh + dot_nt(er_in[...], f_gr[...]))
+    mg_out[...] = jnp.transpose(d_mesh + dot_nt(er_in[...], whole(f_gr)))
     arrive(dgrid_copies)
-    dpre_out[...] = (dot(f_gs[...], dgrid_in[...]) * sgrid[:, at(c, gb)]).astype(bf16)
+    dpre_out[...] = (dot(whole(f_gs), dgrid_in[...]) * sgrid[:, at(c, gb)]).astype(bf16)
     dpre_copies = swap_rows(dpre_out, dpre_in)
     arrive(mo_copies)
     mesh_out[...] = mo_in[...]
     arrive(dpre_copies)
 
-    part[...] = dot_nt(gpad[...], dpre_in[...]).astype(bf16)
-    piece = part.shape[0] // inner
-    first = []
-    for k in range(1, inner):
-        q = lax.rem(place + k, inner)
-        first.append(remote(part.at[at(q, piece), :], rs1.at[place], {"band": inner_peers[k - 1]}))
+    share_rows, piece = part.shape[0] // 2, part.shape[0] // inner
+    part[at(1 - core, share_rows), :] = dot_nt(gpad[at(1 - core, share_rows), :], dpre_in[...]).astype(bf16)
+    pair = send([(part.at[at(1 - core, share_rows), :], pair_in, {"band": sibling})], pair_in)
     mg_copies = swap_rows(mg_out, mg_in)
-    rs1[place] = part[at(place, piece), :]
+    mine_half = dot_nt(gpad[at(core, share_rows), :], dpre_in[...])
+    arrive(pair)
+    pair_sum[...] = (mine_half + pair_in[...].astype(f32)).astype(bf16)
+    first = send(
+        [(pair_sum.at[at(p, piece), :], rs1.at[row], {"band": b}) for p, b in zip(row_peers, inner_peers)],
+        rs1.at[: rows - 1],
+    )
+    rs1[row] = pair_sum[at(row, piece), :]
     arrive(first)
     mine[...] = jnp.sum(rs1[...].astype(f32), axis=0)
+    second = send([(mine, rs2.at[group], {"band": b}) for b in outer_peers], rs2.at[: outer - 1])
     rs2[group] = mine[...]
-    second = [remote(mine, rs2.at[group], {"band": b}) for b in outer_peers]
     arrive(mg_copies)
     mesh_grad[...] = mg_in[...]
     arrive(second)
-    last[...] = (jnp.sum(rs2[...], axis=0) * scale).astype(bf16)
-    total[at(place, piece), :] = last[...]
-    third = [remote(last, total.at[at(place, piece), :], {"band": b}) for b in inner_peers]
+    own = at(core * rows + row, piece)
+    total[own, :] = (jnp.sum(rs2[...], axis=0) * scale).astype(bf16)
+    third = send([(total.at[own, :], total.at[own, :], {"band": b}) for b in inner_peers], total.at[: (rows - 1) * piece, :])
     arrive(third)
-    w_grid_grad[...] = total[0:fin, :].astype(f32)
-    for copy in started:
-        copy.wait_send()
+    done = total.at[at(core, share_rows), :]
+    arrive(send([(done, done, {"band": sibling})], done))
+    w_grid_sum[...] = total[...]
+    for batch in list(started):
+        sent(batch)
+
+
+def hand_over(mesh_out_in, mesh_grad_in, w_grid_sum, mesh_out, mesh_grad, w_grid_grad):
+    mesh_out[...] = mesh_out_in[...]
+    mesh_grad[...] = mesh_grad_in[...]
+    w_grid_grad[...] = w_grid_sum[0 : w_grid_grad.shape[0], :].astype(f32)
 
 
 def local(nband, nchan, inner, *args):
@@ -514,7 +591,6 @@
     fp = -(-fin // 128) * 128
     scale = float(grid_dev * nband) ** (-0.5)
     v = pltpu.VMEM
-    full = v((width, width), bf16)
     nodes = v((mesh_dev, cb), bf16)
     block = v((nb, width), bf16)
     held = [
@@ -526,36 +602,46 @@
         v((fp, grid_dev), bf16), v((fp, cb), bf16), v((width, fp), bf16), v((16, cb), f32),
         v((16, edges), bf16), v((16, medges), bf16),
         v((width, mesh_dev), bf16), v((nchan, 8, cb), f32), v((width, nb), bf16),
-        *[full] * 10,
+        v((10, nchan, cb, width), bf16),
         v((width, grid_dev), f32), v((cb, grid_dev), bf16), v((offs, cb, cap), bf16), v((offs * cb, cap), bf16),
         v((cb, edges), f32), v((cb, edges), bf16),
         v((mesh_dev // 2, 2 * cb), f32), nodes, block,
         block, block, nodes, nodes, v((cb, mesh_dev), bf16), v((offs, cb, mcap), bf16), v((offs * cb, mcap), bf16),
         v((cb, medges), f32), v((cb, medges), bf16), nodes, block,
-        v((width, nb), bf16), v((cb, mesh_dev), bf16), block, nodes, v((offs * cb, mcap), f32),
+        *[v((width, nb), bf16), v((cb, mesh_dev), bf16)] * 2, v((offs * cb, mcap), f32),
         v((offs, cb, mcap), bf16), v((offs, cb, mcap), bf16), nodes, block, nodes, block,
-        block, nodes, v((offs * cb, cap), f32), v((offs, cb, cap), bf16), v((offs, cb, cap), bf16), nodes, block,
+        v((width, nb), bf16), v((cb, mesh_dev), bf16), v((offs * cb, cap), f32), v((offs, cb, cap), bf16), v((offs, cb, cap), bf16), nodes, block,
         v((width, nb), f32), v((cb, mesh_dev), f32),
         v((cb, grid_dev), bf16), v((width, gb), bf16), v((width, gb), bf16), v((cb, grid_dev), bf16),
-        v((fp, cb), bf16), v((inner, fp // inner, cb), bf16), v((fp // inner, cb), f32),
-        v((nband // inner, fp // inner, cb), f32), v((fp // inner, cb), bf16), v((fp, cb), bf16),
-        pltpu.SemaphoreType.DMA((SEMS,)), pltpu.SemaphoreType.DMA((SEMS,)), pltpu.SemaphoreType.DMA((32,)),
+        v((fp, cb), bf16), v((fp // 2, cb), bf16), v((fp // 2, cb), bf16), v((inner // 2, fp // inner, cb), bf16),
+        v((fp // inner, cb), f32), v((nband // inner, fp // inner, cb), f32), v((fp, cb), bf16),
+        pltpu.SemaphoreType.DMA((BATCHES,)), pltpu.SemaphoreType.DMA((BATCHES,)), pltpu.SemaphoreType.DMA((OWN,)),
     ]
-    spec = pl.BlockSpec(memory_space=pltpu.VMEM)
-    return pl.pallas_call(
+    spec, anywhere = pl.BlockSpec(memory_space=pltpu.VMEM), pl.BlockSpec(memory_space=pl.ANY)
+    results = pl.pallas_call(
         functools.partial(kernel, nband, nchan, inner, scale),
         out_shape=(
             jax.ShapeDtypeStruct((cb, mesh_dev), bf16),
             jax.ShapeDtypeStruct((cb, mesh_dev), f32),
-            jax.ShapeDtypeStruct((fin, cb), f32),
+            jax.ShapeDtypeStruct((fp, cb), bf16),
         ),
-        in_specs=[pl.BlockSpec(memory_space=pl.ANY)] * len(names),
+        in_specs=[anywhere] * len(names),
         out_specs=(spec,) * 3,
         scratch_shapes=scratch,
         compiler_params=pltpu.CompilerParams(
             collective_id=0, has_side_effects=True, vmem_limit_bytes=56 * 2**20
         ),
     )(*[a[name] for name in names])
+    return pl.pallas_call(
+        hand_over,
+        out_shape=(
+            jax.ShapeDtypeStruct((cb, mesh_dev), bf16),
+            jax.ShapeDtypeStruct((cb, mesh_dev), f32),
+            jax.ShapeDtypeStruct((fin, cb), f32),
+        ),
+        in_specs=[spec] * 3,
+        out_specs=(spec,) * 3,
+    )(*results)
 
 
 def solution(mesh):

time: 131 us -> 121 us (0.924)
  Pallas kernels: 127 us -> 121 us
  local copies, waits for them, and re-layouts: 3.34 us -> 0 us
    pallas_call x1, Pallas kernels: 127 us -> 119 us  [local(): pl.pallas_call(functools.partial(kernel, nband, nchan, inner, scale), out...]
    unnamed x7 -> x0, local copies, waits for them, and re-layouts: 3.34 us -> none
    pallas_call x0 -> x1, Pallas kernels: none -> 1.89 us  [local(): pl.pallas_call(hand_over, out_shape=(jax.ShapeDtypeStruct((cb, mesh_dev),...]
where the time goes in v2:
time: 121 us
  Pallas kernels  121 us (100%)
    pallas_call x1, Pallas kernels, local(): pl.pallas_call(functools.partial(kernel, nband, nchan, inner, scale), out...  119 us

profile of v2, /device:TPU:1, one launch (start us, length us, event | category | flops | bytes accessed | tf_op | source)
XLA Modules:
  0.0 121.2 jit_solution(13270927386269123914)
XLA Ops:
  0.6 118.6 %shard_map.265 = (bf16[128,512]{1,0:T(8,128)(2,1)}, f32[128,512]{1,0:T(8,128)}, bf16[512,128]{1,0:T(8,128)(2,1)}) custom-call(bf16[474,1024]{1,0:T(8,128)(2,1)} %grid_hbm.1, bf16[474,128]{1,0:T(8,128)(2,1)} %w_grid_hbm.1, bf16[128,512]{1,0:T(8,128)(2,1)} %mesh_in.1, bf16[4,8192]{1,0:T(4,128)(2,1)} %g2m_attr_hbm.1, s32[5,512]{1,0:T(8,128)} %g2m_send_hbm.1, ...), custom_call_target="tpu_custom_call" | custom-call | tf_op jit(solution)/shard_map/pallas_call | solution.py:621
  119.3 1.9 %shard_map.266 = (bf16[128,512]{1,0:T(8,128)(2,1)}, f32[128,512]{1,0:T(8,128)}, f32[474,128]{1,0:T(8,128)}) custom-call(bf16[128,512]{1,0:T(8,128)(2,1)} %get-tuple-element.6.mesh_out_in, f32[128,512]{1,0:T(8,128)} %get-tuple-element.7.mesh_grad_in, bf16[512,128]{1,0:T(8,128)(2,1)} %get-tuple-element.8.w_grid_sum), custom_call_target="tpu_custom_call" | custom-call | tf_op jit(solution)/shard_map/pallas_call | solution.py:635

commit v3 on v2

--- a/solution.py
+++ b/solution.py
@@ -11,7 +11,7 @@
 bf16 = jnp.bfloat16
 f32 = jnp.float32
 MESH = pl.DeviceIdType.MESH
-BATCHES, OWN = 40, 22
+BATCHES, OWN = 42, 25
 INPUTS = (
     *("grid_in", "w_grid", "mesh_in", "g2m_attr", "g2m_send", "g2m_src", "g2m_dst"),
     *("w_gs", "w_gr", "w_ge", "w_nm", "w_na", "w_no", "gain_enc"),
@@ -215,7 +215,7 @@
     def wg_half(p):
         return wg_t.at[at(2 * p + core, cb // 2), :]
 
-    wg_copies = to_chan(lambda p: wg_half(c), wg_half(c), wg_t.at[: others * cb // 2, :])
+    wg_copies = [send([(wg_half(c), wg_half(c), {"chan": p})], wg_half(c)) for p in chan_peers]
     gains[c] = jnp.zeros(gains.shape[1:], f32)
 
     gpad[tail:, :] = jnp.zeros((gpad.shape[0] - tail, grid_dev), bf16)
@@ -226,7 +226,8 @@
     own_mesh.wait()
     for copy in own_rest:
         copy.wait()
-    sent(wg_copies)
+    for batch in wg_copies:
+        sent(batch)
     mesh_copies = to_chan(lambda p: mesh_in, mesh_full.at[at(c, cb), :], mesh_full.at[: others * cb, :])
     gains[c, 0:1, :] = gain_enc[...]
     gains[c, 1:2, :] = gain_proc[...]
@@ -240,40 +241,16 @@
     attr_m[...] = jnp.zeros_like(attr_m)
     attr_m[0:ea, :] = mesh_attr[...]
     wgr_t = flip(w_gr[...]).astype(bf16)
-    arrive(wg_copies)
-    halves = [wg_half(p) for p in chan_peers]
-    arrive(send([(half_block, half_block, {"band": sibling}) for half_block in halves], wg_t.at[: others * cb // 2, :]))
-
-    step = min(256, grid_dev)
-
-    @pl.loop(0, grid_dev // step)
-    def _(t):
-        cols = at(t, step)
-        pre = dot(wg_t[...], gpad[:, cols])
-        sig = sigmoid(pre)
-        sgrid[:, cols] = sig * (1.0 + pre * (1.0 - sig))
-        s_grid[:, cols] = dot(wgs_t, (pre * sig).astype(bf16)).astype(bf16)
-
-    order = [j for o in range(radius, 0, -1) for j in (radius - o, radius + o)]
-    passes = [order[i : i + 2] for i in range(0, len(order), 2)]
-
-    def pack(field, lists, out, dest):
-        def picked(j):
-            return dot(field[...], one_hot(lists[j : j + 1, :], field.shape[1])).astype(bf16)
-
-        def block(j):
-            return dest.at[j * cb : (j + 1) * cb, :]
-
-        def sends():
-            for j in order:
-                out[j] = picked(j)
-                yield out.at[j], block(j), {"band": band_at(j - radius)}
-
-        batch = send(sends(), dest.at[: (offs - 1) * cb, :])
-        dest[radius * cb : (radius + 1) * cb, :] = picked(radius)
-        return batch
-
-    halo = pack(s_grid, g2m_send, halo_out, table)
+
+    def passed_on():
+        for batch, k in zip(wg_copies, far_first(nchan)[::-1]):
+            arrive(batch)
+            piece = wg_half(lax.rem(c - k + nchan, nchan))
+            yield piece, piece, {"band": sibling}
+
+
+    wg_copies.reverse()
+    wg_shared = send(passed_on(), wg_t.at[: others * cb // 2, :])
 
     def part_of(shard, full, cuts):
         index = group if cuts > 1 else 0
@@ -335,6 +312,40 @@
     gain_copies = to_chan(lambda p: gains.at[c], gains.at[c], gains.at[:others])
     group_m = fetch([(w_ms, f_ms), (w_mr, f_mr)], outer)
     group_a = fetch([(w_nm, f_nm), (w_na, f_na), (w_no, f_no)])
+
+    arrive(wg_shared)
+
+    step = min(512, grid_dev)
+
+    @pl.loop(0, grid_dev // step)
+    def _(t):
+        cols = at(t, step)
+        pre = dot(wg_t[...], gpad[:, cols])
+        sig = sigmoid(pre)
+        sgrid[:, cols] = sig * (1.0 + pre * (1.0 - sig))
+        s_grid[:, cols] = dot(wgs_t, (pre * sig).astype(bf16)).astype(bf16)
+
+    order = [j for o in range(radius, 0, -1) for j in (radius - o, radius + o)]
+    passes = [order[i : i + 2] for i in range(0, len(order), 2)]
+
+    def pack(field, lists, out, dest):
+        def picked(j):
+            return dot(field[...], one_hot(lists[j : j + 1, :], field.shape[1])).astype(bf16)
+
+        def block(n):
+            return dest.at[n * cb : (n + 1) * cb, :]
+
+        def sends():
+            for n, j in enumerate(order):
+                out[j] = picked(j)
+                yield out.at[j], block(n), {"band": band_at(j - radius)}
+
+        batch = send(sends(), dest.at[: (offs - 1) * cb, :])
+        dest[len(order) * cb :, :] = picked(radius)
+        return batch
+
+    halo = pack(s_grid, g2m_send, halo_out, table)
+
     group_b = fetch([(w_pm, f_pm), (w_pa, f_pa), (w_po, f_po)], outer)
     group_c = fetch([(w_gr, f_gr), (w_gs, f_gs)], outer)
 
@@ -350,7 +361,7 @@
             cols = at(t, tile)
             slot, low = slots_of(src[:, cols], table.shape[1], offs)
             upper, node = halves_of(dst[:, cols], half)
-            own = dot(table[radius * cb : (radius + 1) * cb, :], one_hot(low, table.shape[1]))
+            own = dot(table[len(order) * cb :, :], one_hot(low, table.shape[1]))
             pre = jnp.where(slot == radius, own, 0.0) + dot(w_edge_t, attr[:, cols])
             grads[:, cols] = pre + pick_half(upper, dot(recv, one_hot(node, half)))
 
@@ -362,13 +373,10 @@
             cols = at(t, tile)
             slot, low = slots_of(src[:, cols], table.shape[1], offs)
             upper, node = halves_of(dst[:, cols], half)
-            by_src = one_hot(low, table.shape[1])
-            below = dot(table[: radius * cb, :], by_src)
-            above = dot(table[(radius + 1) * cb :, :], by_src)
+            remote = dot(table[: len(order) * cb, :], one_hot(low, table.shape[1]))
             sender = jnp.zeros((cb, tile), f32)
-            for j in range(radius):
-                sender = jnp.where(slot == j, below[j * cb : (j + 1) * cb, :], sender)
-                sender = jnp.where(slot == j + radius + 1, above[j * cb : (j + 1) * cb, :], sender)
+            for n, j in enumerate(order):
+                sender = jnp.where(slot == j, remote[n * cb : (n + 1) * cb, :], sender)
             pre = grads[:, cols] + sender
             sig = sigmoid(pre)
             grads[:, cols] = sig * (1.0 + pre * (1.0 - sig))
@@ -537,7 +545,7 @@
     dpre_out[...] = (dot(whole(f_gs), dgrid_in[...]) * sgrid[:, at(c, gb)]).astype(bf16)
     dpre_copies = swap_rows(dpre_out, dpre_in)
     arrive(mo_copies)
-    mesh_out[...] = mo_in[...]
+    outputs = [fetch_local(mo_in, mesh_out)]
     arrive(dpre_copies)
 
     share_rows, piece = part.shape[0] // 2, part.shape[0] // inner
@@ -557,7 +565,7 @@
     second = send([(mine, rs2.at[group], {"band": b}) for b in outer_peers], rs2.at[: outer - 1])
     rs2[group] = mine[...]
     arrive(mg_copies)
-    mesh_grad[...] = mg_in[...]
+    outputs.append(fetch_local(mg_in, mesh_grad))
     arrive(second)
     own = at(core * rows + row, piece)
     total[own, :] = (jnp.sum(rs2[...], axis=0) * scale).astype(bf16)
@@ -565,15 +573,34 @@
     arrive(third)
     done = total.at[at(core, share_rows), :]
     arrive(send([(done, done, {"band": sibling})], done))
-    w_grid_sum[...] = total[...]
+    outputs.append(fetch_local(total, w_grid_sum))
     for batch in list(started):
         sent(batch)
-
-
-def hand_over(mesh_out_in, mesh_grad_in, w_grid_sum, mesh_out, mesh_grad, w_grid_grad):
-    mesh_out[...] = mesh_out_in[...]
-    mesh_grad[...] = mesh_grad_in[...]
-    w_grid_grad[...] = w_grid_sum[0 : w_grid_grad.shape[0], :].astype(f32)
+    for copy in outputs:
+        copy.wait()
+
+
+def hand_over(
+    mesh_out_in, mesh_grad_in, w_grid_sum, mesh_out, mesh_grad, w_grid_grad,
+    held_out, held_grad, held_sum, held_w, sems,
+):
+    def copy(i, src, dst):
+        started = pltpu.make_async_copy(src, dst, sems.at[i])
+        started.start()
+        return started
+
+    grad_in = copy(0, mesh_grad_in, held_grad)
+    sum_in = copy(1, w_grid_sum, held_sum)
+    out_in = copy(2, mesh_out_in, held_out)
+    grad_in.wait()
+    grad_out = copy(3, held_grad, mesh_grad)
+    sum_in.wait()
+    held_w[...] = held_sum[0 : held_w.shape[0], :].astype(f32)
+    w_out = copy(4, held_w, w_grid_grad)
+    out_in.wait()
+    out_out = copy(5, held_out, mesh_out)
+    for last in (grad_out, w_out, out_out):
+        last.wait()
 
 
 def local(nband, nchan, inner, *args):
@@ -617,7 +644,7 @@
         v((fp // inner, cb), f32), v((nband // inner, fp // inner, cb), f32), v((fp, cb), bf16),
         pltpu.SemaphoreType.DMA((BATCHES,)), pltpu.SemaphoreType.DMA((BATCHES,)), pltpu.SemaphoreType.DMA((OWN,)),
     ]
-    spec, anywhere = pl.BlockSpec(memory_space=pltpu.VMEM), pl.BlockSpec(memory_space=pl.ANY)
+    anywhere = pl.BlockSpec(memory_space=pl.ANY)
     results = pl.pallas_call(
         functools.partial(kernel, nband, nchan, inner, scale),
         out_shape=(
@@ -626,7 +653,7 @@
             jax.ShapeDtypeStruct((fp, cb), bf16),
         ),
         in_specs=[anywhere] * len(names),
-        out_specs=(spec,) * 3,
+        out_specs=(anywhere,) * 3,
         scratch_shapes=scratch,
         compiler_params=pltpu.CompilerParams(
             collective_id=0, has_side_effects=True, vmem_limit_bytes=56 * 2**20
@@ -639,8 +666,12 @@
             jax.ShapeDtypeStruct((cb, mesh_dev), f32),
             jax.ShapeDtypeStruct((fin, cb), f32),
         ),
-        in_specs=[spec] * 3,
-        out_specs=(spec,) * 3,
+        in_specs=[anywhere] * 3,
+        out_specs=(anywhere,) * 3,
+        scratch_shapes=[
+            v((cb, mesh_dev), bf16), v((cb, mesh_dev), f32), v((fp, cb), bf16), v((fin, cb), f32),
+            pltpu.SemaphoreType.DMA((6,)),
+        ],
     )(*results)
 
 

time: 121 us -> 120 us (level)
  Pallas kernels: 121 us -> 119 us
where the time goes in v3:
time: 120 us
  Pallas kernels  119 us (99%)
    pallas_call x1, Pallas kernels, local(): pl.pallas_call(functools.partial(kernel, nband, nchan, inner, scale), out...  118 us

profile of v3, /device:TPU:1, one launch (start us, length us, event | category | flops | bytes accessed | tf_op | source)
XLA Modules:
  0.0 120.3 jit_solution(18402927692224954904)
XLA Ops:
  0.6 117.6 %shard_map.265 = (bf16[128,512]{1,0:T(8,128)(2,1)}, f32[128,512]{1,0:T(8,128)}, bf16[512,128]{1,0:T(8,128)(2,1)}) custom-call(bf16[474,1024]{1,0:T(8,128)(2,1)} %grid_hbm.1, bf16[474,128]{1,0:T(8,128)(2,1)} %w_grid_hbm.1, bf16[128,512]{1,0:T(8,128)(2,1)} %mesh_in.1, bf16[4,8192]{1,0:T(4,128)(2,1)} %g2m_attr_hbm.1, s32[5,512]{1,0:T(8,128)} %g2m_send_hbm.1, ...), custom_call_target="tpu_custom_call" | custom-call | tf_op jit(solution)/shard_map/pallas_call | solution.py:648
  118.3 1.8 %shard_map.266 = (bf16[128,512]{1,0:T(8,128)(2,1)}, f32[128,512]{1,0:T(8,128)}, f32[474,128]{1,0:T(8,128)}) custom-call(bf16[128,512]{1,0:T(8,128)(2,1)} %get-tuple-element.6.mesh_out_in, f32[128,512]{1,0:T(8,128)} %get-tuple-element.7.mesh_grad_in, bf16[512,128]{1,0:T(8,128)(2,1)} %get-tuple-element.8.w_grid_sum), custom_call_target="tpu_custom_call" | custom-call | tf_op jit(solution)/shard_map/pallas_call | solution.py:662

commit v4 on v3

--- a/solution.py
+++ b/solution.py
@@ -387,7 +387,7 @@
         out[half:, :] = acc[:, cb:].astype(bf16)
 
     def edges_backward(grad, src, dst, grads, back, rows_ref, out, inbound, tile):
-        capacity, tiles = rows_ref.shape[1], src.shape[1] // tile
+        capacity, tiles = rows_ref.shape[0], src.shape[1] // tile
         acc[...] = jnp.zeros_like(acc)
         rows_ref[...] = jnp.zeros_like(rows_ref)
         copies = []
@@ -396,9 +396,8 @@
             slot, low = slots_of(src[:, cols], capacity, offs)
             slot = slot.astype(jnp.int16)
             parts = [jnp.where(slot == j, d_pre, jnp.zeros((), bf16)) for j in slots]
-            rows_ref[base : base + len(slots) * cb, :] += dot_nt(
-                jnp.concatenate(parts, axis=0) if len(parts) > 1 else parts[0], one_hot(low, capacity)
-            )
+            parts = jnp.concatenate(parts, axis=0) if len(parts) > 1 else parts[0]
+            rows_ref[:, base : base + len(slots) * cb] += dot_nt(one_hot(low, capacity), parts)
 
         for i, slots in enumerate(passes):
             base = 2 * i * cb
@@ -413,7 +412,7 @@
                 add_rows(slots, base, cols, back[:, cols])
 
             for n, j in enumerate(slots):
-                out[j] = rows_ref[base + n * cb : base + (n + 1) * cb, :].astype(bf16)
+                out[j] = rows_ref[:, base + n * cb : base + (n + 1) * cb].astype(bf16)
             sends = [(out.at[j], inbound.at[j], {"band": band_at(radius - j)}) for j in slots]
             copies.append(send(sends, inbound.at[: len(slots)]))
 
@@ -427,7 +426,7 @@
             acc[...] += dot_nt(one_hot(node, half), upper_lower(upper, d_pre.astype(f32)))
             add_rows([radius], base, cols, d_pre)
 
-        inbound[radius] = rows_ref[base : base + cb, :].astype(bf16)
+        inbound[radius] = rows_ref[:, base : base + cb].astype(bf16)
         return copies
 
     tile_g = min(4096, g2m_src.shape[1])
@@ -513,7 +512,7 @@
         return value
 
     h_out[...] = gather_back(
-        m_back, m_back_in, lambda j, rows: dot_nt(one_hot(mesh_send[j : j + 1, :], mesh_dev), rows)
+        m_back, m_back_in, lambda j, rows: dot(one_hot(mesh_send[j : j + 1, :], mesh_dev), rows)
     ).astype(bf16)
     h_copies = swap_rows(h_out, h_in)
     arrive(mr_copies)
@@ -536,13 +535,13 @@
     er_copies = swap_rows(er_out, er_in)
     arrive(c_copies)
     dgrid_out[...] = gather_back(
-        g_back, g_back_in, lambda j, rows: dot_nt(rows, one_hot(g2m_send[j : j + 1, :], grid_dev))
+        g_back, g_back_in, lambda j, rows: dot(one_hot(g2m_send[j : j + 1, :], grid_dev), rows)
     ).astype(bf16)
-    dgrid_copies = swap_lanes(dgrid_out, dgrid_in)
+    dgrid_copies = swap_rows(dgrid_out, dgrid_in)
     arrive(er_copies)
     mg_out[...] = jnp.transpose(d_mesh + dot_nt(er_in[...], whole(f_gr)))
     arrive(dgrid_copies)
-    dpre_out[...] = (dot(whole(f_gs), dgrid_in[...]) * sgrid[:, at(c, gb)]).astype(bf16)
+    dpre_out[...] = (dot_nt(whole(f_gs), dgrid_in[...]) * sgrid[:, at(c, gb)]).astype(bf16)
     dpre_copies = swap_rows(dpre_out, dpre_in)
     arrive(mo_copies)
     outputs = [fetch_local(mo_in, mesh_out)]
@@ -635,11 +634,11 @@
         v((mesh_dev // 2, 2 * cb), f32), nodes, block,
         block, block, nodes, nodes, v((cb, mesh_dev), bf16), v((offs, cb, mcap), bf16), v((offs * cb, mcap), bf16),
         v((cb, medges), f32), v((cb, medges), bf16), nodes, block,
-        *[v((width, nb), bf16), v((cb, mesh_dev), bf16)] * 2, v((offs * cb, mcap), f32),
-        v((offs, cb, mcap), bf16), v((offs, cb, mcap), bf16), nodes, block, nodes, block,
-        v((width, nb), bf16), v((cb, mesh_dev), bf16), v((offs * cb, cap), f32), v((offs, cb, cap), bf16), v((offs, cb, cap), bf16), nodes, block,
+        *[v((width, nb), bf16), v((cb, mesh_dev), bf16)] * 2, v((mcap, offs * cb), f32),
+        v((offs, mcap, cb), bf16), v((offs, mcap, cb), bf16), nodes, block, nodes, block,
+        v((width, nb), bf16), v((cb, mesh_dev), bf16), v((cap, offs * cb), f32), v((offs, cap, cb), bf16), v((offs, cap, cb), bf16), nodes, block,
         v((width, nb), f32), v((cb, mesh_dev), f32),
-        v((cb, grid_dev), bf16), v((width, gb), bf16), v((width, gb), bf16), v((cb, grid_dev), bf16),
+        v((grid_dev, cb), bf16), v((gb, width), bf16), v((width, gb), bf16), v((cb, grid_dev), bf16),
         v((fp, cb), bf16), v((fp // 2, cb), bf16), v((fp // 2, cb), bf16), v((inner // 2, fp // inner, cb), bf16),
         v((fp // inner, cb), f32), v((nband // inner, fp // inner, cb), f32), v((fp, cb), bf16),
         pltpu.SemaphoreType.DMA((BATCHES,)), pltpu.SemaphoreType.DMA((BATCHES,)), pltpu.SemaphoreType.DMA((OWN,)),

time: 120 us -> 120 us (level)
  no operation moved by 1% of the time
where the time goes in v4:
time: 120 us
  Pallas kernels  119 us (99%)
    pallas_call x1, Pallas kernels, local(): pl.pallas_call(functools.partial(kernel, nband, nchan, inner, scale), out...  117 us

profile of v4, /device:TPU:1, one launch (start us, length us, event | category | flops | bytes accessed | tf_op | source)
XLA Modules:
  0.0 119.9 jit_solution(16263487556061955578)
XLA Ops:
  0.6 117.3 %shard_map.265 = (bf16[128,512]{1,0:T(8,128)(2,1)}, f32[128,512]{1,0:T(8,128)}, bf16[512,128]{1,0:T(8,128)(2,1)}) custom-call(bf16[474,1024]{1,0:T(8,128)(2,1)} %grid_hbm.1, bf16[474,128]{1,0:T(8,128)(2,1)} %w_grid_hbm.1, bf16[128,512]{1,0:T(8,128)(2,1)} %mesh_in.1, bf16[4,8192]{1,0:T(4,128)(2,1)} %g2m_attr_hbm.1, s32[5,512]{1,0:T(8,128)} %g2m_send_hbm.1, ...), custom_call_target="tpu_custom_call" | custom-call | tf_op jit(solution)/shard_map/pallas_call | solution.py:647
  117.9 1.8 %shard_map.266 = (bf16[128,512]{1,0:T(8,128)(2,1)}, f32[128,512]{1,0:T(8,128)}, f32[474,128]{1,0:T(8,128)}) custom-call(bf16[128,512]{1,0:T(8,128)(2,1)} %get-tuple-element.6.mesh_out_in, f32[128,512]{1,0:T(8,128)} %get-tuple-element.7.mesh_grad_in, bf16[512,128]{1,0:T(8,128)(2,1)} %get-tuple-element.8.w_grid_sum), custom_call_target="tpu_custom_call" | custom-call | tf_op jit(solution)/shard_map/pallas_call | solution.py:661
